TPU v7x, 256 devices: a whole 4x4x8 slice. The times are simulated.
256 devices in a mesh: replica: 4 (over z_lo), shard: 64 (over y, x, z_hi, core).
Axes of the slice: x: 4, y: 4, z: 8 (z_hi: 2, z_lo: 4; z = z_hi * 4 + z_lo), core: 2. Of those that a mesh axis runs over, the one named last changes fastest.
Arguments:
- hidden: bfloat16 [2, 49152, 7168], P(None, ('replica', 'shard')), may hold values from -6 to 6
- norm_gains: bfloat16 [2, 7168], P(None, 'shard'), may hold values from 0.5 to 1.5
- head_block: bfloat16 [256, 7168], P('shard'), may hold values from -0.21875 to 0.21875
- targets: int32 [2, 49152], P(None, ('replica', 'shard')), may hold values from 0 to 511
- rest_lse: float32 [2, 49152], P(None, ('replica', 'shard')), may hold values from 8 to 12
- cotangent: float32 [2, 49152], P(None, ('replica', 'shard')), may hold values from 0.5 to 5
Outputs:
- grad_hidden: bfloat16 [2, 49152, 7168], P(None, ('replica', 'shard'))
- grad_head: float32 [256, 7168], P('shard')
- grad_gains: float32 [2, 7168], P(None, 'shard')
All inputs are finite; a program needn't handle non-finite values.
Results may differ from a plain program's by a relative error of at most 0.0063.
Values may be sent and summed in bfloat16 or wider, within the bound.
A program may use at most 128 MiB of HBM per device.

v0:
```python
import jax
import jax.numpy as jnp
from jax import lax
from jax.sharding import PartitionSpec as P

eps = 1e-06


def local(hidden, norm_gains, head_block, targets, rest_lse, cotangent):
    head, gains = (
        lax.all_gather(head_block, "shard", axis=0, tiled=True),
        lax.all_gather(norm_gains, "shard", axis=1, tiled=True),
    )
    vocab = head.shape[0]
    xf = hidden.astype(jnp.float32)
    scale = lax.rsqrt(jnp.mean(xf * xf, axis=-1) + eps)
    gainf = gains.astype(jnp.float32)
    normed = (xf * scale[..., None] * gainf[:, None, :]).astype(jnp.bfloat16)
    rows = hidden.shape[0] * hidden.shape[1]
    flat = normed.reshape(rows, hidden.shape[2])
    logits = lax.dot_general(
        flat, head, (((1,), (1,)), ((), ())), preferred_element_type=jnp.float32
    )
    total = jnp.log(jnp.exp(rest_lse.reshape(rows)) + jnp.sum(jnp.exp(logits), axis=-1))
    column = jnp.arange(vocab, dtype=jnp.int32)
    onehot = (targets.reshape(rows)[:, None] == column[None, :]).astype(jnp.float32)
    dlogits = (
        cotangent.reshape(rows)[:, None] * (jnp.exp(logits - total[:, None]) - onehot)
    ).astype(jnp.bfloat16)
    dnormed = jnp.dot(dlogits, head, preferred_element_type=jnp.float32).reshape(xf.shape)
    inner = jnp.mean(xf * gainf[:, None, :] * dnormed, axis=-1)
    grad_x = scale[..., None] * gainf[:, None, :] * dnormed - xf * (scale**3 * inner)[..., None]
    grad_hidden = grad_x.astype(jnp.bfloat16)
    gain_part = jnp.sum(dnormed * xf * scale[..., None], axis=1)
    gain_owned = lax.psum_scatter(gain_part, "shard", scatter_dimension=1, tiled=True)
    owned = lax.psum_scatter(
        lax.dot_general(
            dlogits, flat, (((0,), (0,)), ((), ())), preferred_element_type=jnp.float32
        ),
        "shard",
        scatter_dimension=0,
        tiled=True,
    )
    grad_head, grad_gains = lax.psum((owned, gain_owned), "replica")
    return (grad_hidden, grad_head, grad_gains)


def solution(mesh):
    in_specs = (
        P(None, ("replica", "shard"), None),
        P(None, "shard"),
        P("shard", None),
        P(None, ("replica", "shard")),
        P(None, ("replica", "shard")),
        P(None, ("replica", "shard")),
    )
    out_specs = (P(None, ("replica", "shard"), None), P("shard", None), P(None, "shard"))
    return jax.shard_map(local, mesh=mesh, in_specs=in_specs, out_specs=out_specs, check_vma=False)
```

profile of v0, /device:TPU:1, one launch (start us, length us, event | category | flops | bytes accessed | tf_op | source)
XLA Modules:
  0.0 1461.6 jit_solution(18284744392917955108)
XLA Ops:
  7.2 0.0 all-gather.4.cloned.1.call-start
  7.2 0.7 all-gather.4.cloned.1.call-update
  7.9 0.0 all-reduce.6.cloned.1.call-start
  7.9 0.8 eq.15
  8.7 0.8 mul.78
  9.5 0.7 exp.16
  10.2 0.1 exp.17
  10.2 123.1 %all-gather = bf16[64,112,2]{1,2,0:T(2,128)(2,1)S(1)} all-gather(bf16[1,112,2]{1,2,0:T(2,128)(2,1)} %bitcast.30), channel_id=1, replica_groups=mesh['replica'=4,'shard'=64] {'shard'}, dimensions={0}, use_global_device_ids=true | all-gather | bytes 29120 | tf_op jit(solution)/shard_map/all_gather | solution.py:12
  133.4 0.1 reshape.45
  133.5 0.0 copy-start.1
  133.5 3.9 fusion
  137.4 0.3 copy-done.1
  137.7 4.2 fusion.2
  141.9 0.0 slice-start.2
  141.9 0.0 all-gather.4.cloned.1.call-done
  141.9 6.8 reshape.44
  148.8 0.0 slice-start.3
  148.8 5.9 exponential_reduce_fusion
  154.7 0.0 slice-done.2
  154.7 0.0 slice-done.3
  154.7 0.0 copy-start.2
  154.7 5.1 fusion.10
  159.8 0.0 slice-start
  159.8 0.0 all-reduce.6.cloned.1.call-update
  159.8 0.0 reduce-scatter.4.cloned.1.call-start
  159.9 0.0 copy-done.2
  159.9 0.6 dynamic-slice
  161.1 0.0 slice-start.1
  161.1 3.9 fusion.11
  165.0 0.0 copy-start
  165.0 0.0 slice-done
  165.0 0.0 slice-done.1
  165.0 3.8 fusion.8
  168.8 0.3 copy-done
  169.1 2.4 copy.12
  171.5 0.0 reduce-scatter.4.cloned.1.call-update
  171.6 0.2 all-reduce.4.cloned.1.call-start
  171.8 819.1 %all-reduce.6.cloned.1.call-done = f32[256,7168]{1,0:T(8,128)} async-done(((f32[256,7168]{1,0:T(8,128)}), f32[256,7168]{1,0:T(8,128)}) %all-reduce.6.cloned.1.call-update) | async-done | bytes 7340048
  990.9 1.6 constant_dynamic-slice_fusion
  992.5 0.0 all-reduce.4.cloned.1.call-update
  992.5 11.5 fusion.6
  1004.0 398.6 %reduce-scatter.4.cloned.1.call-done = f32[112,2]{1,0:T(8,128)} async-done(((f32[7168,2]{1,0:T(8,128)}), f32[112,2]{1,0:T(8,128)}) %reduce-scatter.4.cloned.1.call-update) | async-done | bytes 912
  1402.6 0.9 copy.13
  1403.5 10.6 psum.15
  1414.2 39.4 %all-reduce.4.cloned.1.call-done = f32[4,7168]{1,0:T(4,128)} async-done(((f32[4,7168]{1,0:T(4,128)}), f32[4,7168]{1,0:T(4,128)}) %all-reduce.4.cloned.1.call-update) | async-done | bytes 114704 | tf_op jit(solution)/shard_map/psum | solution.py:44
  1453.5 1.6 copy.17
  (6 shorter events, 0.0 us)
Async XLA Ops:
  7.2 134.8 %all-gather.4.cloned.1.call-start = ((), (), s32[]{:S(2)}) async-start(), calls=%async_computation.2 | async-start | bytes 3727360 | tf_op jit(solution)/shard_map/all_gather | solution.py:11
  7.9 983.0 %all-reduce.6.cloned.1.call-start = ((), (), s32[]{:S(2)}) async-start(), calls=%async_computation.4 | async-start | bytes 14680064
  133.5 4.2 copy-start.1
  141.9 12.8 slice-start.2
  148.8 5.9 slice-start.3
  154.7 5.2 copy-start.2
  159.8 5.2 slice-start
  159.8 1242.8 %reduce-scatter.4.cloned.1.call-start = ((), (), s32[]{:S(2)}) async-start(), calls=%async_computation.3 | async-start | bytes 3727360
  161.1 3.9 slice-start.1
  165.0 4.2 copy-start
  171.6 1282.0 %all-reduce.4.cloned.1.call-start = ((), (), s32[]{:S(2)}) async-start(), calls=%async_computation.1 | async-start | bytes 229376 | tf_op jit(solution)/shard_map/psum | solution.py:44
Sparse Core Ops, SparseCore 0:
  11.5 94.4 all-gather.3
  159.9 830.8 all-reduce.5
  993.5 409.0 reduce-scatter.3
  1405.7 47.7 all-reduce.3
where the time goes:
time: 1460 us
  waiting for transfers between devices  1260 us (86%)
  blocking collectives  134 us (9%)
  other arithmetic  23.4 us (2%)
  local copies, waits for them, and re-layouts  16.9 us (1%)
  matrix products  14.8 us (1%)
    unnamed x6, waiting for transfers between devices  1220 us
    all_gather x1, blocking collectives, local(): lax.all_gather(norm_gains, 'shard', axis=1, tiled=True)  123 us
    psum x1, waiting for transfers between devices, local(): grad_head, grad_gains = lax.psum((owned, gain_owned), 'replica')  39.4 us
  transfers between devices with their start and end apart: 4, of which 3 were waited for; matrix products, arithmetic and copies ran while one was open for 2% of the time, Pallas kernels for 0%

commit v1 on v0

v1 whole, which is shorter than its diff:
```python
import jax
import jax.numpy as jnp
from jax import lax
from jax.experimental import pallas as pl
from jax.experimental.pallas import tpu as pltpu
from jax.sharding import PartitionSpec as P

eps = 1e-06
F32, BF16, I32 = jnp.float32, jnp.bfloat16, jnp.int32
MESH = pl.DeviceIdType.MESH

D = 7168
HALF = D // 2
G = 896
W = 2 * G
V = 256
T = 384
RT = 32
NRT = T // RT
GN = 112
NSEM = 160


def iota(shape, dim):
    return lax.broadcasted_iota(I32, shape, dim)


def kernel(
    hid_ref, gain_ref, head_ref, tgt_ref, rest_ref, cot_ref,
    gx_ref, gw_ref, gg_ref,
    xv, nv, hv, r_own, r_sib, raw, gcol, gblk, gfull, scale_v,
    dl_t, dl_v, coef_v, dn_v, gacc, p_scr, xs, xr, s0, s1, f0, f1, n0, n1,
    t0, t1, fb0, fb1, nb0, nb1, zsum, zp, zr, yv, fr,
    local_sem, send_sem, recv_sem, zsend_sem, zrecv_sem, fsend_sem, frecv_sem,
):
    zl = lax.axis_index("replica")
    shard = lax.axis_index("shard")
    c = shard & 1
    zh = (shard >> 1) & 1
    x = (shard >> 2) & 3
    y = shard >> 4
    z = zh * 4 + zl
    pc = x + c * (y - x)
    qc = y + c * (x - y)

    def device(q, p, zz, cc):
        xx = p + c * (q - p)
        yy = q + c * (p - q)
        return (zz & 3, ((yy * 4 + xx) * 2 + (zz >> 2)) * 2 + cc)

    def at(dq=0, dp=0):
        return device((qc + dq) & 3, (pc + dp) & 3, z, c)

    sibling = (zl, shard + 1 - 2 * c)

    count = [0]
    started = []

    def send(src, dst, target, start=True):
        i = count[0]
        count[0] += 1
        copy = pltpu.make_async_remote_copy(
            src_ref=src, dst_ref=dst, send_sem=send_sem.at[i], recv_sem=recv_sem.at[i],
            device_id=target, device_id_type=MESH,
        )
        if start:
            copy.start()
            started.append(copy)
        return copy

    loads = []
    for i in range(4):
        rows = pl.ds(i * 96, 96)
        copy = pltpu.make_async_copy(hid_ref.at[rows], xv.at[rows], local_sem.at[i])
        copy.start()
        loads.append(copy)

    partners = [sibling]
    for d in (1, 2, 3):
        partners += [at(dq=d), at(dp=d)]
    for d in range(1, 8):
        partners.append(device(qc, pc, (z + d) & 7, c))
    for d in range(1, 4):
        partners.append(device(qc, pc, zh * 4 + ((zl + d) & 3), 1 - c))
    barrier = pltpu.get_barrier_semaphore()
    for partner in partners:
        pl.semaphore_signal(barrier, inc=1, device_id=partner, device_id_type=MESH)

    hb = head_ref[...].astype(F32)
    for h in range(2):
        parts = [hb[:, (h * 4 + f) * G:(h * 4 + f + 1) * G] for f in range(4)]
        raw[h] = jnp.concatenate(parts, axis=0).astype(BF16)
    r_own[qc, pc, zh, c] = raw[c]
    gpad = jnp.concatenate([gain_ref[...].astype(F32), jnp.zeros((2, 128 - GN), F32)], axis=1)
    gcol[zh * 2 + c] = jnp.concatenate([gpad, jnp.zeros((6, 128), F32)], axis=0)

    pl.semaphore_wait(barrier, len(partners))

    w = zh * 2 + c
    m_g = send(gcol.at[w], gcol.at[w], sibling)
    m_h = send(raw.at[1 - c], r_own.at[pc, qc, zh, c], sibling)
    edge = (zl == 0) | (zl == 3)
    step = jnp.where(zl == 3, 1, -1)
    m_g.wait_recv()
    z_gain = [
        send(gcol.at[pl.ds(zh * 2, 2)], gcol.at[pl.ds(zh * 2, 2)],
             device(qc, pc, (z + d * step) & 7, c), start=False)
        for d in (1, 2)
    ]

    @pl.when(edge)
    def _():
        for copy in z_gain:
            copy.start()

    m_h.wait_recv()

    def block(q, p, k):
        return r_own.at[q & 3, p & 3, k]

    own = {}

    def spread(k, name, q, p, piece=None):
        ref = block(q, p, k)
        own[name, "q+"] = send(ref, ref, at(dq=1))
        own[name, "q-"] = send(ref, ref, at(dq=-1))

    def begin(k, n):
        ref = block(qc, pc, k)
        own[n, "p+"] = send(ref, ref, at(dp=1))
        own[n, "p-"] = send(ref, ref, at(dp=-1))
        spread(k, (n, 0), qc, pc)

    def p_near(k, n):
        own[n, "p+"].wait_recv()
        ref = block(qc, pc - 1, k).at[0]
        own[n, "pf+"] = send(ref, ref, at(dp=1))
        spread(k, (n, -1), qc, pc - 1)
        own[n, "p-"].wait_recv()
        ref = block(qc, pc + 1, k).at[1]
        own[n, "pf-"] = send(ref, ref, at(dp=-1))
        spread(k, (n, 1), qc, pc + 1)

    def p_far(k, n):
        own[n, "pf+"].wait_recv()
        own[n, "pf-"].wait_recv()
        spread(k, (n, 2), qc, pc + 2)

    def to_sibling(k, n, q):
        ref = r_own.at[q & 3, :, k]
        own[n, "sib", count[0]] = copy = send(ref, r_sib.at[q & 3, :, k], sibling)
        return copy

    def q_forward(k, n, b):
        own[(n, b), "q+"].wait_recv()
        ref = block(qc - 1, pc + b, k).at[0]
        own[(n, b), "qf+"] = send(ref, ref, at(dq=1))
        own[(n, b), "q-"].wait_recv()
        ref = block(qc + 1, pc + b, k).at[1]
        own[(n, b), "qf-"] = send(ref, ref, at(dq=-1))

    def q_far(k, n):
        for b in (0, -1, 1, 2):
            own[(n, b), "qf+"].wait_recv()
            own[(n, b), "qf-"].wait_recv()

    def scale_tiles(first, last):
        def body(i, carry):
            rows = pl.ds(pl.multiple_of(i * RT, RT), RT)
            total = jnp.zeros((RT, 128), F32)
            for j in range(D // G):
                part = xv[rows, j * G:(j + 1) * G].astype(F32)
                part = part * part
                for l in range(G // 128):
                    total += part[:, l * 128:(l + 1) * 128]
            mean = jnp.sum(total, axis=1, keepdims=True) * (1.0 / D)
            scale_v[rows] = jnp.broadcast_to(lax.rsqrt(mean + eps), (RT, 128))
            return carry
        lax.fori_loop(first, last, body, 0)

    def lanes(v):
        return jnp.concatenate([v] * (G // 128), axis=1)

    def normed_tiles(first, last):
        def body(i, carry):
            rows = pl.ds(pl.multiple_of(i * RT, RT), RT)
            k = jnp.where(i >= NRT // 2, 1, 0)
            s = lanes(scale_v[rows])
            for j in range(D // G):
                cols = slice(j * G, (j + 1) * G)
                g = gfull[k, :, cols]
                g = jnp.concatenate([g] * (RT // 8), axis=0)
                nv[rows, cols] = (xv[rows, cols].astype(F32) * s * g).astype(BF16)
            return carry
        lax.fori_loop(first, last, body, 0)

    def pieces(rows, shift):
        r = iota((rows, G), 0)
        p = (r >> shift) & 3
        q = r >> (shift + 2)
        return r, p + c * (q - p), q + c * (p - q)

    def spread_matrix():
        j = iota((128, G), 0)
        col = iota((128, G), 1)
        hit = jnp.zeros((128, G), jnp.bool_)
        for m in range(8):
            hit = hit | (col == j + GN * m)
        return jnp.where(hit & (j < GN), 1.0, 0.0).astype(BF16)

    def inside(rows, shift, w_of):
        r, xx, _ = pieces(rows, shift)
        m = (xx & 1) * 4 + w_of(r)
        col = iota((rows, G), 1)
        return (col >= m * GN) & (col < (m + 1) * GN)

    def make_gains():
        lhs = gblk[...].reshape(128, 128).astype(BF16)
        u = jnp.dot(lhs, spread_matrix(), preferred_element_type=F32)
        u = jnp.where(inside(128, 3, lambda r: (r >> 1) & 3), u, 0.0).astype(BF16)
        o = iota((16, 128), 0)
        i = iota((16, 128), 1)
        p = (i >> 3) & 3
        q = i >> 5
        xx = p + c * (q - p)
        yy = q + c * (p - q)
        sel = ((yy * 2 + (xx >> 1)) == (o >> 1)) & ((i & 1) == (o & 1))
        full = jnp.dot(jnp.where(sel, 1.0, 0.0).astype(BF16), u, preferred_element_type=F32)
        for j in range(8):
            for k in range(2):
                row = full[2 * j + k:2 * j + k + 1]
                gfull[k, :, j * G:(j + 1) * G] = jnp.broadcast_to(row, (8, G))

    def permutation():
        o = iota((V, V), 0)
        i = iota((V, V), 1)
        src = ((o >> 4) & 3) * 64 + ((o >> 2) & 3) * 16 + (o >> 6) * 4 + (o & 3)
        return jnp.where(i == src, 1.0, 0.0).astype(BF16)

    def place(buf, half, core, q):
        q = q & 3
        rows = jnp.dot(permutation(), buf[q].reshape(V, G), preferred_element_type=F32).astype(BF16)
        for f in range(4):
            cols = pl.ds(pl.multiple_of(half * HALF + f * G, 128), G)
            for p in range(4):
                yy = q + core * (p - q)
                xx = p + core * (q - p)
                hv[yy * 4 + xx, :, cols] = rows[f * 64 + p * 16:f * 64 + (p + 1) * 16]

    begin(zh, 0)
    z_head = [
        send(block(qc, pc, zh), block(qc, pc, zh), device(qc, pc, (z + d * step) & 7, c), start=False)
        for d in (1, 2)
    ]

    @pl.when(edge)
    def _():
        for copy in z_head:
            copy.start()

    def z_arrives(copies):
        @pl.when(edge)
        def _():
            copies[0].wait_recv()

        @pl.when(jnp.logical_not(edge))
        def _():
            copies[1].wait_recv()

    z_arrives(z_gain)
    gblk[qc, pc] = jnp.concatenate([gcol[i][0:2] for i in range(4)], axis=0)
    g_p = [send(gblk.at[qc, pc], gblk.at[qc, pc], at(dp=d)) for d in (1, -1, 2)]
    for copy in loads:
        copy.wait()
    scale_tiles(0, 3)
    p_near(zh, 0)
    z_arrives(z_head)
    begin(1 - zh, 1)
    for copy in g_p:
        copy.wait_recv()
    g_q = [send(gblk.at[qc], gblk.at[qc], at(dq=d)) for d in (1, -1, 2)]
    scale_tiles(3, 6)
    p_far(zh, 0)
    q_forward(zh, 0, 0)
    scale_tiles(6, 9)
    p_near(1 - zh, 1)
    q_forward(zh, 0, -1)
    q_forward(zh, 0, 1)
    scale_tiles(9, 12)
    p_far(1 - zh, 1)
    to_sibling(zh, 0, qc)
    for copy in g_q:
        copy.wait_recv()
    make_gains()
    q_forward(zh, 0, 2)
    q_forward(1 - zh, 1, 0)
    sib = [to_sibling(zh, 0, qc + 1), to_sibling(zh, 0, qc - 1), to_sibling(1 - zh, 1, qc)]
    normed_tiles(0, 6)
    q_forward(1 - zh, 1, -1)
    q_forward(1 - zh, 1, 1)
    q_far(zh, 0)
    to_sibling(zh, 0, qc + 2)
    q_forward(1 - zh, 1, 2)
    to_sibling(1 - zh, 1, qc + 1)
    to_sibling(1 - zh, 1, qc - 1)
    normed_tiles(6, 12)
    place(r_own, c, c, qc)
    place(r_own, c, c, qc + 1)
    place(r_own, c, c, qc - 1)
    q_far(1 - zh, 1)
    to_sibling(1 - zh, 1, qc + 2)
    place(r_own, c, c, qc + 2)

    def logits_part(half):
        total = None
        for j in range(2):
            cols = pl.ds(pl.multiple_of(half * HALF + j * W, 128), W)
            part = lax.dot_general(
                hv[:, :, cols].reshape(V, W), nv[:, cols],
                (((1,), (1,)), ((), ())), preferred_element_type=F32)
            total = part if total is None else total + part
        return total

    first_half = logits_part(c)
    for key in list(own):
        if key[1] == "sib":
            own[key].wait_recv()
    for q in range(4):
        place(r_sib, 1 - c, 1 - c, q)
    logits = first_half + logits_part(1 - c)

    def row(ref):
        return jnp.concatenate([ref[0:1], ref[1:2]], axis=1)

    total = jnp.log(jnp.exp(row(rest_ref)) + jnp.sum(jnp.exp(logits), axis=0, keepdims=True))
    onehot = jnp.where(row(tgt_ref) == iota((V, T), 0), 1.0, 0.0)
    grad = (row(cot_ref) * (jnp.exp(logits - total) - onehot)).astype(BF16)
    dl_t[...] = grad
    grad = grad.astype(F32)
    inner = jnp.sum(grad * logits, axis=0, keepdims=True) * (1.0 / D)

    def partial(half, j):
        for i in range(2):
            cols = pl.ds(pl.multiple_of(half * HALF + j * W + i * G, 128), G)
            p_scr[:, :, i * G:(i + 1) * G] = jnp.dot(
                dl_t[...], nv[:, cols], preferred_element_type=F32).reshape(16, 16, G)

    def give(j):
        partial(1 - c, j)

        def body(b, carry):
            xs[j, b] = p_scr[b].astype(BF16)
            return carry
        lax.fori_loop(0, 16, body, 0)
        return send(xs.at[j], xr.at[j], sibling)

    def take(j, copy, s):
        copy.wait_recv()

        def body(b, carry):
            q, p = b >> 2, b & 3
            yy = q + c * (p - q)
            xx = p + c * (q - p)
            both = p_scr[yy * 4 + xx] + xr[j, yy * 4 + xx].astype(F32)
            s[q, p, :, 0:W] = both.astype(BF16)
            return carry
        lax.fori_loop(0, 16, body, 0)

    def ring_begin(s, width, f, n, hop, here, rows_of):
        lo, hi = slice(0, G), slice(G, width)
        far, up, down = (here + 2) & 3, (here + 1) & 3, (here - 1) & 3
        m = {}
        m["f+"] = send(rows_of(s, far, lo), f[0], hop(1))
        m["f-"] = send(rows_of(s, far, hi), f[1], hop(-1))
        m["n+"] = send(rows_of(s, up, hi), rows_of(n, 0, hi), hop(1))
        m["n-"] = send(rows_of(s, down, lo), rows_of(n, 1, lo), hop(-1))
        return m

    def ring_join(m, s, width, f, n, hop, here, rows_of):
        lo, hi = slice(0, G), slice(G, width)
        up, down = (here + 1) & 3, (here - 1) & 3
        m["f+"].wait_recv()
        ref = rows_of(s, up, lo)
        ref[...] = (ref[...].astype(F32) + f[0][...].astype(F32)).astype(BF16)
        m["j+"] = send(ref, rows_of(n, 0, lo), hop(1))
        m["f-"].wait_recv()
        ref = rows_of(s, down, hi)
        ref[...] = (ref[...].astype(F32) + f[1][...].astype(F32)).astype(BF16)
        m["j-"] = send(ref, rows_of(n, 1, hi), hop(-1))

    def ring_end(m):
        for name in ("n+", "n-", "j+", "j-"):
            m[name].wait_recv()

    def slab(ref, i, cols):
        return ref.at[i, :, :, cols]

    def tile(ref, i, cols):
        return ref.at[i, :, cols]

    def hop_q(d):
        return at(dq=d)

    def hop_p(d):
        return at(dp=d)

    big = [(s0, W, (f0.at[0], f0.at[1]), n0), (s1, W + 128, (f1.at[0, :, :, 0:G], f1.at[1]), n1)]
    small = [(t0, W, (fb0.at[0], fb0.at[1]), nb0), (t1, W + 128, (fb1.at[0, :, 0:G], fb1.at[1]), nb1)]

    def big_end(j, m):
        ring_end(m)
        s, _, _, n = big[j]
        t = small[j][0]

        def body(p, carry):
            t[p] = (s[qc, p].astype(F32) + n[0, p].astype(F32) + n[1, p].astype(F32)).astype(BF16)
            return carry
        lax.fori_loop(0, 4, body, 0)

    def small_end(j, m):
        ring_end(m)
        t, width, _, n = small[j]
        zsum[:, 0:width] = t[pc].astype(F32) + n[0].astype(F32) + n[1].astype(F32)
        for owner in range(4):
            rows = slice(owner * 4, owner * 4 + 4)
            zp[j, owner, :, 0:G] = jnp.concatenate([zsum[rows, 0:G], zsum[rows, G:W]], axis=0)
            if j == 1:
                zp[j, owner, :, G:G + 128] = zsum[0:8, W:W + 128]
        for owner in range(4):
            target = (owner >> 1) * 4 + (owner & 1) * 2 + j
            copy = z_copy(j, owner)

            @pl.when(target != z)
            def _():
                copy.start()

            @pl.when(target == z)
            def _():
                zr[z, :, 0:G + 128 * j] = zp[j, owner, :, 0:G + 128 * j]

    def z_copy(j, owner):
        wide = G + 128 * j
        target = (owner >> 1) * 4 + (owner & 1) * 2 + j
        return pltpu.make_async_remote_copy(
            src_ref=zp.at[j, owner, :, 0:wide], dst_ref=zr.at[z, :, 0:wide],
            send_sem=zsend_sem.at[j, owner], recv_sem=zrecv_sem.at[z],
            device_id=device(qc, pc, target, c), device_id_type=MESH,
        )

    def f_copy(to):
        return pltpu.make_async_remote_copy(
            src_ref=yv, dst_ref=fr.at[c, zl & 1],
            send_sem=fsend_sem.at[to], recv_sem=frecv_sem.at[c * 2 + (zl & 1)],
            device_id=device(qc, pc, zh * 4 + to, zl >> 1), device_id_type=MESH,
        )

    def z_end(j):
        wide = G + 128 * j

        @pl.when((zl & 1) == j)
        def _():
            for src in range(8):
                @pl.when(src != z)
                def _():
                    pltpu.make_async_remote_copy(
                        src_ref=zp.at[j, 0, :, 0:wide], dst_ref=zr.at[src, :, 0:wide],
                        send_sem=zsend_sem.at[j, 0], recv_sem=zrecv_sem.at[src],
                        device_id=sibling, device_id_type=MESH,
                    ).wait_recv()
            total = zr[0, :, 0:wide]
            for src in range(1, 8):
                total = total + zr[src, :, 0:wide]
            yv[:, 0:wide] = total
            if j == 0:
                yv[:, G:G + 128] = jnp.zeros((8, 128), F32)
            for to in range(4):
                mine = (zl == to) & (c == (zl >> 1))

                @pl.when(jnp.logical_not(mine))
                def _():
                    f_copy(to).start()

                @pl.when(mine)
                def _():
                    fr[c, zl & 1] = yv[...]

    def hidden_block(j):
        cols = pl.ds(pl.multiple_of(j * G, 128), G)
        dn_v[...] = jnp.dot(dl_v[...], hv[:, :, cols].reshape(V, G), preferred_element_type=F32)
        for k in range(2):
            def body(i, acc):
                rows = pl.ds(pl.multiple_of(i * RT, RT), RT)
                s = lanes(scale_v[rows])
                g = jnp.concatenate([gfull[k, :, cols]] * (RT // 8), axis=0)
                xf = xv[rows, cols].astype(F32)
                dn = dn_v[rows]
                sdn = s * dn
                xv[rows, cols] = (g * sdn - xf * lanes(coef_v[rows])).astype(BF16)
                prod = sdn * xf
                for r in range(RT // 8):
                    acc = acc + prod[r * 8:(r + 1) * 8]
                return acc
            acc = lax.fori_loop(k * NRT // 2, (k + 1) * NRT // 2, body, jnp.zeros((8, G), F32))
            gacc[j * 2 + k] = acc

    outs = []

    def hidden_out(j):
        cols = pl.ds(pl.multiple_of(j * G, 128), G)
        copy = pltpu.make_async_copy(xv.at[:, cols], gx_ref.at[:, cols], local_sem.at[4 + j])
        copy.start()
        outs.append(copy)

    def rider():
        full = jnp.concatenate(
            [jnp.sum(gacc[i], axis=0, keepdims=True) for i in range(16)], axis=0).astype(BF16)
        o = iota((V, 16), 0)
        i = iota((V, 16), 1)
        p = (o >> 4) & 3
        q = o >> 6
        xx = p + c * (q - p)
        yy = q + c * (p - q)
        sel = ((yy * 2 + (xx >> 1)) == (i >> 1)) & ((o & 1) == (i & 1)) & ((o & 15) < 8)
        u = jnp.dot(jnp.where(sel, 1.0, 0.0).astype(BF16), full, preferred_element_type=F32)
        u = jnp.where(inside(V, 4, lambda r: (r >> 1) & 3), u, 0.0).astype(BF16)
        out = lax.dot_general(
            u, spread_matrix(), (((1,), (1,)), ((), ())), preferred_element_type=F32)
        s1[:, :, :, W:W + 128] = out.astype(BF16).reshape(4, 4, 16, 128)

    give0 = give(0)
    partial(c, 0)
    take(0, give0, s0)
    b0 = ring_begin(s0, W, big[0][2], n0, hop_q, qc, slab)
    dl_v[...] = jnp.transpose(dl_t[...].astype(F32)).astype(BF16)
    coef = jnp.transpose(jnp.broadcast_to(inner, (128, T)))
    sc = scale_v[...]
    coef_v[...] = coef * sc * sc
    for j in range(3):
        hidden_block(j)
        hidden_out(j)
    ring_join(b0, s0, W, big[0][2], n0, hop_q, qc, slab)
    give1 = give(1)
    for j in range(3, 8):
        hidden_block(j)
        hidden_out(j)
    rider()
    partial(c, 1)
    take(1, give1, s1)
    b1 = ring_begin(s1, W + 128, big[1][2], n1, hop_q, qc, slab)
    big_end(0, b0)
    c0 = ring_begin(t0, W, small[0][2], nb0, hop_p, pc, tile)
    ring_join(b1, s1, W + 128, big[1][2], n1, hop_q, qc, slab)
    ring_join(c0, t0, W, small[0][2], nb0, hop_p, pc, tile)
    small_end(0, c0)
    big_end(1, b1)
    c1 = ring_begin(t1, W + 128, small[1][2], nb1, hop_p, pc, tile)
    z_end(0)
    ring_join(c1, t1, W + 128, small[1][2], nb1, hop_p, pc, tile)
    small_end(1, c1)
    z_end(1)

    for src in range(2):
        for ch in range(2):
            mine = (c == src) & (zl == c * 2 + ch)

            @pl.when(jnp.logical_not(mine))
            def _():
                pltpu.make_async_remote_copy(
                    src_ref=yv, dst_ref=fr.at[src, ch],
                    send_sem=fsend_sem.at[0], recv_sem=frecv_sem.at[src * 2 + ch],
                    device_id=sibling, device_id_type=MESH,
                ).wait_recv()
            for sub in range(2):
                first = src * HALF + ch * W + sub * G
                gw_ref[:, first:first + G] = fr[src, ch, sub * 4:sub * 4 + 4, 0:G]
    gains = fr[0, 1, :, G:G + 128] + fr[1, 1, :, G:G + 128]
    mine = jnp.zeros((2, 128), F32)
    for i in range(4):
        mine = jnp.where(w == i, gains[i * 2:i * 2 + 2], mine)
    gg_ref[...] = mine[:, 0:GN]

    for copy in started:
        copy.wait_send()

    @pl.when(edge)
    def _():
        for copy in z_gain + z_head:
            copy.wait_send()
    for j in range(2):
        for owner in range(4):
            target = (owner >> 1) * 4 + (owner & 1) * 2 + j

            @pl.when(target != z)
            def _():
                z_copy(j, owner).wait_send()
    for to in range(4):
        @pl.when(jnp.logical_not((zl == to) & (c == (zl >> 1))))
        def _():
            f_copy(to).wait_send()
    for copy in outs:
        copy.wait()


def local(hidden, norm_gains, head_block, targets, rest_lse, cotangent):
    any_space = pl.BlockSpec(memory_space=pl.ANY)
    vmem = pl.BlockSpec(memory_space=pltpu.VMEM)
    scratch = [
        pltpu.VMEM((T, D), BF16),
        pltpu.VMEM((T, D), BF16),
        pltpu.VMEM((16, 16, D), BF16),
        pltpu.VMEM((4, 4, 2, 2, 16, G), BF16),
        pltpu.VMEM((4, 4, 2, 2, 16, G), BF16),
        pltpu.VMEM((2, 16, G), BF16),
        pltpu.VMEM((4, 8, 128), F32),
        pltpu.VMEM((4, 4, 8, 128), F32),
        pltpu.VMEM((2, 8, D), F32),
        pltpu.VMEM((T, 128), F32),
        pltpu.VMEM((V, T), BF16),
        pltpu.VMEM((T, V), BF16),
        pltpu.VMEM((T, 128), F32),
        pltpu.VMEM((T, G), F32),
        pltpu.VMEM((16, 8, G), F32),
        pltpu.VMEM((16, 16, W), F32),
        pltpu.VMEM((2, 16, 16, W), BF16),
        pltpu.VMEM((2, 16, 16, W), BF16),
        pltpu.VMEM((4, 4, 16, W), BF16),
        pltpu.VMEM((4, 4, 16, W + 128), BF16),
        pltpu.VMEM((2, 4, 16, G), BF16),
        pltpu.VMEM((2, 4, 16, G + 128), BF16),
        pltpu.VMEM((2, 4, 16, W), BF16),
        pltpu.VMEM((2, 4, 16, W + 128), BF16),
        pltpu.VMEM((4, 16, W), BF16),
        pltpu.VMEM((4, 16, W + 128), BF16),
        pltpu.VMEM((2, 16, G), BF16),
        pltpu.VMEM((2, 16, G + 128), BF16),
        pltpu.VMEM((2, 16, W), BF16),
        pltpu.VMEM((2, 16, W + 128), BF16),
        pltpu.VMEM((16, W + 128), F32),
        pltpu.VMEM((2, 4, 8, G + 128), F32),
        pltpu.VMEM((8, 8, G + 128), F32),
        pltpu.VMEM((8, G + 128), F32),
        pltpu.VMEM((2, 2, 8, G + 128), F32),
        pltpu.SemaphoreType.DMA((12,)),
        pltpu.SemaphoreType.DMA((NSEM,)),
        pltpu.SemaphoreType.DMA((NSEM,)),
        pltpu.SemaphoreType.DMA((2, 4)),
        pltpu.SemaphoreType.DMA((8,)),
        pltpu.SemaphoreType.DMA((4,)),
        pltpu.SemaphoreType.DMA((4,)),
    ]
    grad_hidden, grad_head, grad_gains = pl.pallas_call(
        kernel,
        out_shape=(
            jax.ShapeDtypeStruct((T, D), BF16),
            jax.ShapeDtypeStruct((4, D), F32),
            jax.ShapeDtypeStruct((2, GN), F32),
        ),
        in_specs=[any_space, vmem, vmem, vmem, vmem, vmem],
        out_specs=(any_space, vmem, vmem),
        scratch_shapes=scratch,
        compiler_params=pltpu.CompilerParams(
            collective_id=0, has_side_effects=True, vmem_limit_bytes=60 << 20),
        cost_estimate=pl.CostEstimate(
            flops=6 * T * D * V, bytes_accessed=4 * T * D, transcendentals=2 * T * V),
        name="head_backward",
    )(hidden.reshape(T, D), norm_gains, head_block, targets, rest_lse, cotangent)
    return grad_hidden.reshape(hidden.shape), grad_head, grad_gains


def solution(mesh):
    tokens = P(None, ("replica", "shard"))
    in_specs = (
        P(None, ("replica", "shard"), None),
        P(None, "shard"),
        P("shard", None),
        tokens,
        tokens,
        tokens,
    )
    out_specs = (P(None, ("replica", "shard"), None), P("shard", None), P(None, "shard"))
    return jax.shard_map(local, mesh=mesh, in_specs=in_specs, out_specs=out_specs, check_vma=False)
```

time: 1460 us -> 86.4 us (0.06)
  waiting for transfers between devices: 1260 us -> 0 us
  blocking collectives: 134 us -> 0 us
  Pallas kernels: 0 us -> 79 us
  other arithmetic: 23.4 us -> 0 us
  matrix products: 14.8 us -> 0 us
    unnamed x6 -> x0, waiting for transfers between devices: 1220 us -> none
    all_gather x1 -> x0, blocking collectives: 123 us -> none  [local(): lax.all_gather(norm_gains, 'shard', axis=1, tiled=True)]
    pallas_call x0 -> x1, Pallas kernels: none -> 79 us  [local(): pl.pallas_call(kernel, out_shape=(jax.ShapeDtypeStruct((T, D), BF16), jax...]
    psum x1 -> x0, waiting for transfers between devices: 39.4 us -> none  [local(): grad_head, grad_gains = lax.psum((owned, gain_owned), 'replica')]
    convert_element_type x3 -> x0, other arithmetic: 15.7 us -> none  [the longest x1 11.5 us: local(): grad_hidden = grad_x.astype(jnp.bfloat16)]
    dot_general x3 -> x0, matrix products: 14.8 us -> none  [the longest x1 5.9 us: local(): lax.dot_general(flat, head, (((1,), (1,)), ((), ())), preferred_element_t...]
  transfers between devices with their start and end apart: 4 -> 0, of which waited for: 3 -> 0; matrix products, arithmetic and copies ran while one was open for 2% -> 0% of each run, Pallas kernels for 0% -> 0%
where the time goes in v1:
time: 86.4 us; the launch traced here: 86.2 us
  Pallas kernels  79 us (91%)
  local copies, waits for them, and re-layouts  6.61 us (8%)
    pallas_call x1, Pallas kernels, local(): pl.pallas_call(kernel, out_shape=(jax.ShapeDtypeStruct((T, D), BF16), jax...  79 us
    unnamed x7, local copies, waits for them, and re-layouts  6.61 us

profile of v1, /device:TPU:1, one launch (start us, length us, event | category | flops | bytes accessed | tf_op | source)
XLA Modules:
  0.0 86.2 jit_solution(14709485860975007810)
XLA Ops:
  0.6 79.0 %head_backward.1 = (bf16[384,7168]{1,0:T(8,128)(2,1)}, f32[4,7168]{1,0:T(4,128)}, f32[2,112]{1,0:T(2,128)}) custom-call(bf16[384,7168]{1,0:T(8,128)(2,1)} %bitcast.3, bf16[2,112]{1,0:T(2,128)(2,1)} %gain_ref.1, bf16[4,7168]{1,0:T(4,128)(2,1)} %head_ref.1, s32[2,192]{1,0:T(2,128)} %tgt_ref.1, f32[2,192]{1,0:T(2,128)} %rest_ref.1, f32[2,192]{1,0:T(2,128)} %cot_ref.1), custom_call_target="tpu_custom_call" | custom-call | flops 4227858432 | bytes 11010048 | tf_op jit(solution)/shard_map/head_backward/pallas_call | solution.py:651
  79.6 0.0 copy-start
  79.6 0.0 copy-start.1
  79.6 5.4 %copy.12 = bf16[2,192,7168]{2,1,0:T(8,128)(2,1)} copy(bf16[2,192,7168]{2,1,0:T(8,128)(2,1)} %bitcast.2) | data formatting | bytes 11010048
  85.0 0.0 copy-done
  85.0 0.6 copy.13
  85.7 0.0 copy-done.1
  85.7 0.6 copy.14
Async XLA Ops:
  79.6 5.4 %copy-start = (f32[4,7168]{1,0:T(4,128)S(1)}, f32[4,7168]{1,0:T(4,128)}, u32[]{:S(2)}) copy-start(f32[4,7168]{1,0:T(4,128)} %get-tuple-element.13) | copy-start | bytes 344068
  79.6 6.1 %copy-start.1 = (f32[2,112]{1,0:T(2,128)S(1)}, f32[2,112]{1,0:T(2,128)}, u32[]{:S(2)}) copy-start(f32[2,112]{1,0:T(2,128)} %get-tuple-element.14) | copy-start | bytes 2692

commit v2 on v1

v2 whole, which is shorter than its diff:
```python
import jax
import jax.numpy as jnp
from jax import lax
from jax.experimental import pallas as pl
from jax.experimental.pallas import tpu as pltpu
from jax.sharding import PartitionSpec as P

eps = 1e-06
F32, BF16, I32 = jnp.float32, jnp.bfloat16, jnp.int32
MESH = pl.DeviceIdType.MESH

D = 7168
HALF = D // 2
G = 896
W = 2 * G
GE = G + 128
V = 256
TK = 192
T = 2 * TK
RT = 32
NRT = T // RT
GN = 112
NSEM = 112


def iota(shape, dim):
    return lax.broadcasted_iota(I32, shape, dim)


def kernel(
    hid_ref, gain_ref, head_ref, tgt_ref, rest_ref, cot_ref,
    gx_ref, gw_ref, gg_ref,
    xv, nv, hv, r_own, r_sib, raw, gcol, gblk, gfull, scale_v,
    dl_t, dl_v, coef_v, dn_v, gacc, p_scr, xs, xr, sb, nq, tb, npb,
    zsum, zp, zr, yv, fr,
    local_sem, send_sem, recv_sem, zsend_sem, zrecv_sem, fsend_sem, frecv_sem, near_sem,
):
    zl = lax.axis_index("replica")
    shard = lax.axis_index("shard")
    c = shard & 1
    zh = (shard >> 1) & 1
    x = (shard >> 2) & 3
    y = shard >> 4
    z = zh * 4 + zl
    pc = x + c * (y - x)
    qc = y + c * (x - y)

    def device(q, p, zz, cc):
        xx = p + c * (q - p)
        yy = q + c * (p - q)
        return (zz & 3, ((yy * 4 + xx) * 2 + (zz >> 2)) * 2 + cc)

    def at(dq=0, dp=0):
        return device((qc + dq) & 3, (pc + dp) & 3, z, c)

    def up(dz, cc=c):
        return device(qc, pc, (z + dz) & 7, cc)

    sibling = (zl, shard + 1 - 2 * c)

    count = [0]
    started = []

    def send(src, dst, target, start=True):
        i = count[0]
        count[0] += 1
        copy = pltpu.make_async_remote_copy(
            src_ref=src, dst_ref=dst, send_sem=send_sem.at[i], recv_sem=recv_sem.at[i],
            device_id=target, device_id_type=MESH,
        )
        if start:
            copy.start()
            started.append(copy)
        return copy

    barrier = pltpu.get_barrier_semaphore()
    first = [sibling, at(dp=1), at(dp=-1), at(dq=1), at(dq=-1), up(1), up(-1), up(1, 1 - c), up(-1, 1 - c)]
    for partner in first:
        pl.semaphore_signal(barrier, inc=1, device_id=partner, device_id_type=MESH)

    loads = []
    for i in range(4):
        rows = pl.ds(i * 96, 96)
        copy = pltpu.make_async_copy(hid_ref.at[rows], xv.at[rows], local_sem.at[i])
        copy.start()
        loads.append(copy)

    w = zh * 2 + c
    hb = head_ref[...].astype(F32)
    for h in range(2):
        parts = [hb[:, (h * 4 + f) * G:(h * 4 + f + 1) * G] for f in range(4)]
        raw[h] = jnp.concatenate(parts, axis=0).astype(BF16)
    r_own[qc, pc, zh, c] = raw[c]
    gpad = jnp.concatenate([gain_ref[...].astype(F32), jnp.zeros((2, 128 - GN), F32)], axis=1)
    gcol[w] = jnp.concatenate([gpad, jnp.zeros((6, 128), F32)], axis=0)

    pl.semaphore_wait(barrier, len(first))

    def relay(i, targets):
        for target in targets:
            pl.semaphore_signal(near_sem.at[i], inc=1, device_id=target, device_id_type=MESH)

    relay(0, [at(dp=1), at(dp=-1), at(dq=1), at(dq=-1), up(1), up(-1)])

    edge = (zl == 0) | (zl == 3)
    step = jnp.where(zl == 3, 1, -1)
    m_h = send(raw.at[1 - c], r_own.at[pc, qc, zh, c], sibling)
    m_g = send(gcol.at[w], gcol.at[w], sibling)
    z_head = []
    for d in (1, 2):
        z_head.append([
            send(raw.at[c], r_own.at[qc, pc, zh, c], up(d * step), start=False),
            send(raw.at[1 - c], r_own.at[pc, qc, zh, c], up(d * step, 1 - c), start=False),
        ])

    @pl.when(edge)
    def _():
        for copy in z_head[0]:
            copy.start()

    pl.semaphore_wait(near_sem.at[0], 6)
    relay(1, [up(1), up(-1)])

    @pl.when(edge)
    def _():
        for copy in z_head[1]:
            copy.start()

    def z_arrives(near, far):
        @pl.when(edge)
        def _():
            for copy in near:
                copy.wait_recv()

        @pl.when(jnp.logical_not(edge))
        def _():
            for copy in far:
                copy.wait_recv()

    got = {}

    def along_q(k, dp):
        ref = r_own.at[qc, (pc + dp) & 3, k]
        for d in (1, 3, 2):
            got[k is zh, "q", dp, d] = send(ref, ref, at(dq=d))

    def begin(k):
        ref = r_own.at[qc, pc, k]
        for d in (1, 3, 2):
            got[k is zh, "p", d] = send(ref, ref, at(dp=d))
        along_q(k, 0)

    def p_arrives(k, d):
        got[k is zh, "p", d].wait_recv()
        along_q(k, -d)

    def to_sibling(k, q):
        ref = r_own.at[q & 3, :, k]
        got["sibling", count[0]] = send(ref, r_sib.at[q & 3, :, k], sibling)

    def q_arrives(k, d):
        for dp in (0, -1, -3, -2):
            got[k is zh, "q", dp, d].wait_recv()
        to_sibling(k, qc - d)

    def scale_tiles(begin_tile, end_tile):
        def body(i, carry):
            rows = pl.ds(pl.multiple_of(i * RT, RT), RT)
            total = jnp.zeros((RT, 128), F32)
            for j in range(D // G):
                part = xv[rows, j * G:(j + 1) * G].astype(F32)
                part = part * part
                for l in range(G // 128):
                    total += part[:, l * 128:(l + 1) * 128]
            mean = jnp.sum(total, axis=1, keepdims=True) * (1.0 / D)
            scale_v[rows] = jnp.broadcast_to(lax.rsqrt(mean + eps), (RT, 128))
            return carry
        lax.fori_loop(begin_tile, end_tile, body, 0)

    def lanes(v):
        return jnp.concatenate([v] * (G // 128), axis=1)

    def normed_tiles(begin_tile, end_tile):
        def body(i, carry):
            rows = pl.ds(pl.multiple_of(i * RT, RT), RT)
            k = jnp.where(i >= NRT // 2, 1, 0)
            s = lanes(scale_v[rows])
            for j in range(D // G):
                cols = slice(j * G, (j + 1) * G)
                g = gfull[k, :, cols]
                g = jnp.concatenate([g] * (RT // 8), axis=0)
                nv[rows, cols] = (xv[rows, cols].astype(F32) * s * g).astype(BF16)
            return carry
        lax.fori_loop(begin_tile, end_tile, body, 0)

    def spread_matrix():
        j = iota((128, G), 0)
        col = iota((128, G), 1)
        hit = jnp.zeros((128, G), jnp.bool_)
        for m in range(8):
            hit = hit | (col == j + GN * m)
        return jnp.where(hit & (j < GN), 1.0, 0.0).astype(BF16)

    def inside(rows, shift):
        r = iota((rows, G), 0)
        p = (r >> shift) & 3
        q = r >> (shift + 2)
        xx = p + c * (q - p)
        m = (xx & 1) * 4 + ((r >> 1) & 3)
        col = iota((rows, G), 1)
        return (col >= m * GN) & (col < (m + 1) * GN)

    def make_gains():
        lhs = gblk[...].reshape(128, 128).astype(BF16)
        u = jnp.dot(lhs, spread_matrix(), preferred_element_type=F32)
        u = jnp.where(inside(128, 3), u, 0.0).astype(BF16)
        o = iota((16, 128), 0)
        i = iota((16, 128), 1)
        p = (i >> 3) & 3
        q = i >> 5
        xx = p + c * (q - p)
        yy = q + c * (p - q)
        sel = ((yy * 2 + (xx >> 1)) == (o >> 1)) & ((i & 1) == (o & 1))
        full = jnp.dot(jnp.where(sel, 1.0, 0.0).astype(BF16), u, preferred_element_type=F32)
        for j in range(8):
            for k in range(2):
                row = full[2 * j + k:2 * j + k + 1]
                gfull[k, :, j * G:(j + 1) * G] = jnp.broadcast_to(row, (8, G))

    def permutation():
        o = iota((V, V), 0)
        i = iota((V, V), 1)
        src = ((o >> 4) & 3) * 64 + ((o >> 2) & 3) * 16 + (o >> 6) * 4 + (o & 3)
        return jnp.where(i == src, 1.0, 0.0).astype(BF16)

    def place(buf, half, core, q):
        q = q & 3
        rows = jnp.dot(permutation(), buf[q].reshape(V, G), preferred_element_type=F32).astype(BF16)
        for f in range(4):
            cols = pl.ds(pl.multiple_of(half * HALF + f * G, 128), G)
            for p in range(4):
                yy = q + core * (p - q)
                xx = p + core * (q - p)
                hv[yy * 4 + xx, :, cols] = rows[f * 64 + p * 16:f * 64 + (p + 1) * 16]

    other = 1 - zh
    m_h.wait_recv()
    begin(zh)
    m_g.wait_recv()
    pair = gcol.at[pl.ds(zh * 2, 2)]
    z_gain = [send(pair, pair, up(d * step), start=False) for d in (1, 2)]

    @pl.when(edge)
    def _():
        for copy in z_gain:
            copy.start()

    pl.semaphore_wait(near_sem.at[1], 2)
    relay(2, [up(1), up(-1)])
    loads[0].wait()
    scale_tiles(0, 3)
    for d in (1, 3, 2):
        p_arrives(zh, d)
    to_sibling(zh, qc)
    z_arrives(z_head[0], z_head[1])
    begin(other)
    z_arrives(z_gain[:1], z_gain[1:])
    gblk[qc, pc] = jnp.concatenate([gcol[i][0:2] for i in range(4)], axis=0)
    g_p = [send(gblk.at[qc, pc], gblk.at[qc, pc], at(dp=d)) for d in (1, 3, 2)]
    loads[1].wait()
    scale_tiles(3, 6)
    for d in (1, 3, 2):
        p_arrives(other, d)
    to_sibling(other, qc)
    for copy in g_p:
        copy.wait_recv()
    g_q = [send(gblk.at[qc], gblk.at[qc], at(dq=d)) for d in (1, 3, 2)]
    pl.semaphore_wait(near_sem.at[2], 2)
    loads[2].wait()
    loads[3].wait()
    scale_tiles(6, 12)
    for d in (1, 3, 2):
        q_arrives(zh, d)
    for copy in g_q:
        copy.wait_recv()
    make_gains()
    place(r_own, c, c, qc)
    normed_tiles(0, 6)
    q_arrives(other, 1)
    normed_tiles(6, 12)
    q_arrives(other, 3)
    place(r_own, c, c, qc - 1)
    place(r_own, c, c, qc - 3)
    q_arrives(other, 2)
    place(r_own, c, c, qc - 2)

    def logits_part(half, k):
        total = None
        for j in range(2):
            cols = pl.ds(pl.multiple_of(half * HALF + j * W, 128), W)
            part = lax.dot_general(
                hv[:, :, cols].reshape(V, W), nv[k * TK:(k + 1) * TK, cols],
                (((1,), (1,)), ((), ())), preferred_element_type=F32)
            total = part if total is None else total + part
        return total

    first_half = [logits_part(c, k) for k in range(2)]
    for key in list(got):
        if key[0] == "sibling":
            got[key].wait_recv()
    for q in range(4):
        place(r_sib, 1 - c, 1 - c, q)

    inner = []
    for k in range(2):
        logits = first_half[k] + logits_part(1 - c, k)
        total = jnp.log(jnp.exp(rest_ref[k:k + 1]) + jnp.sum(jnp.exp(logits), axis=0, keepdims=True))
        onehot = jnp.where(tgt_ref[k:k + 1] == iota((V, TK), 0), 1.0, 0.0)
        grad = (cot_ref[k:k + 1] * (jnp.exp(logits - total) - onehot)).astype(BF16)
        dl_t[k] = grad
        inner.append(jnp.sum(grad.astype(F32) * logits, axis=0, keepdims=True) * (1.0 / D))

    def partial(half, s):
        cols = pl.ds(pl.multiple_of(half * HALF + s * G, 128), G)
        for k in range(2):
            p_scr[k] = jnp.dot(
                dl_t[k], nv[k * TK:(k + 1) * TK, cols], preferred_element_type=F32).reshape(16, 16, G)
        return cols

    def fold(v):
        return v[0:8] + v[8:16]

    def give(s):
        cols = partial(1 - c, s)

        def body(b, acc):
            p0, p1 = p_scr[0, b], p_scr[1, b]
            xs[s, b] = (p0 + p1).astype(BF16)
            hf = hv[b, :, cols].astype(F32)
            return acc[0] + fold(hf * p0), acc[1] + fold(hf * p1)
        zero = jnp.zeros((8, G), F32)
        acc = lax.fori_loop(0, 16, body, (zero, zero))
        copy = send(xs.at[s], xr.at[s], sibling)
        for k in range(2):
            gacc[((1 - c) * 4 + s) * 2 + k] = acc[k] / gfull[k, :, cols]
        return copy

    def wide(s):
        return GE if s == 3 else G

    def take(s, copy):
        cols = partial(c, s)
        copy.wait_recv()

        def body(b, acc):
            p, q = b & 3, b >> 2
            yy = q + c * (p - q)
            xx = p + c * (q - p)
            e = yy * 4 + xx
            p0, p1 = p_scr[0, e], p_scr[1, e]
            sb[s, q, p, :, 0:G] = (p0 + p1 + xr[s, e].astype(F32)).astype(BF16)
            hf = hv[e, :, cols].astype(F32)
            return acc[0] + fold(hf * p0), acc[1] + fold(hf * p1)
        zero = jnp.zeros((8, G), F32)
        acc = lax.fori_loop(0, 16, body, (zero, zero))
        for k in range(2):
            gacc[(c * 4 + s) * 2 + k] = acc[k] / gfull[k, :, cols]
        if s == 3:
            rider()
        n = wide(s)
        for d in (2, 1, 3):
            got["rq", s, d] = send(
                sb.at[s, (qc + d) & 3, :, :, 0:n], nq.at[s, d - 1, :, :, 0:n], at(dq=d))

    def q_end(s):
        n = wide(s)
        for d in (1, 3, 2):
            got["rq", s, d].wait_recv()

        def body(p, carry):
            total = sb[s, qc, p, :, 0:n].astype(F32)
            for d in range(3):
                total = total + nq[s, d, p, :, 0:n].astype(F32)
            tb[s, p, :, 0:n] = total.astype(BF16)
            return carry
        lax.fori_loop(0, 4, body, 0)
        for d in (2, 1, 3):
            got["rp", s, d] = send(
                tb.at[s, (pc + d) & 3, :, 0:n], npb.at[s, d - 1, :, 0:n], at(dp=d))

    def p_end(s):
        n = wide(s)
        for d in (1, 3, 2):
            got["rp", s, d].wait_recv()
        total = tb[s, pc, :, 0:n].astype(F32)
        for d in range(3):
            total = total + npb[s, d, :, 0:n].astype(F32)
        zsum[s, :, 0:n] = total

    def z_copy(j, owner):
        n = G + 128 * j
        target = (owner >> 1) * 4 + (owner & 1) * 2 + j
        return pltpu.make_async_remote_copy(
            src_ref=zp.at[j, owner, :, 0:n], dst_ref=zr.at[z, :, 0:n],
            send_sem=zsend_sem.at[j, owner], recv_sem=zrecv_sem.at[z],
            device_id=device(qc, pc, target, c), device_id_type=MESH,
        )

    def z_begin(j):
        n = G + 128 * j
        for owner in range(4):
            rows = slice(owner * 4, owner * 4 + 4)
            zp[j, owner, :, 0:G] = jnp.concatenate(
                [zsum[2 * j, rows, 0:G], zsum[2 * j + 1, rows, 0:G]], axis=0)
            if j == 1:
                zp[j, owner, :, G:GE] = zsum[3, 0:8, G:GE]
        for owner in range(4):
            target = (owner >> 1) * 4 + (owner & 1) * 2 + j
            copy = z_copy(j, owner)

            @pl.when(target != z)
            def _():
                copy.start()

            @pl.when(target == z)
            def _():
                zr[z, :, 0:n] = zp[j, owner, :, 0:n]

    def f_copy(to):
        return pltpu.make_async_remote_copy(
            src_ref=yv, dst_ref=fr.at[c, zl & 1],
            send_sem=fsend_sem.at[to], recv_sem=frecv_sem.at[c * 2 + (zl & 1)],
            device_id=device(qc, pc, zh * 4 + to, zl >> 1), device_id_type=MESH,
        )

    def z_end(j):
        n = G + 128 * j

        @pl.when((zl & 1) == j)
        def _():
            for src in range(8):
                @pl.when(src != z)
                def _():
                    pltpu.make_async_remote_copy(
                        src_ref=zp.at[j, 0, :, 0:n], dst_ref=zr.at[src, :, 0:n],
                        send_sem=zsend_sem.at[j, 0], recv_sem=zrecv_sem.at[src],
                        device_id=sibling, device_id_type=MESH,
                    ).wait_recv()
            total = zr[0, :, 0:n]
            for src in range(1, 8):
                total = total + zr[src, :, 0:n]
            yv[:, 0:n] = total
            if j == 0:
                yv[:, G:GE] = jnp.zeros((8, 128), F32)
            for to in range(4):
                mine = (zl == to) & (c == (zl >> 1))

                @pl.when(jnp.logical_not(mine))
                def _():
                    f_copy(to).start()

                @pl.when(mine)
                def _():
                    fr[c, zl & 1] = yv[...]

    def hidden_block(j):
        cols = slice(j * G, (j + 1) * G)
        dn_v[...] = jnp.dot(dl_v[...], hv[:, :, cols].reshape(V, G), preferred_element_type=F32)
        for k in range(2):
            g = jnp.concatenate([gfull[k, :, cols]] * (RT // 8), axis=0)

            def body(i, carry):
                rows = pl.ds(pl.multiple_of(i * RT, RT), RT)
                gx_ref[rows, cols] = (
                    lanes(scale_v[rows]) * g * dn_v[rows]
                    - xv[rows, cols].astype(F32) * lanes(coef_v[rows])
                ).astype(BF16)
                return carry
            lax.fori_loop(k * NRT // 2, (k + 1) * NRT // 2, body, 0)

    def rider():
        full = jnp.concatenate(
            [jnp.sum(gacc[i], axis=0, keepdims=True) for i in range(16)], axis=0).astype(BF16)
        o = iota((V, 16), 0)
        i = iota((V, 16), 1)
        p = (o >> 4) & 3
        q = o >> 6
        xx = p + c * (q - p)
        yy = q + c * (p - q)
        sel = ((yy * 2 + (xx >> 1)) == (i >> 1)) & ((o & 1) == (i & 1)) & ((o & 15) < 8)
        u = jnp.dot(jnp.where(sel, 1.0, 0.0).astype(BF16), full, preferred_element_type=F32)
        u = jnp.where(inside(V, 4), u, 0.0).astype(BF16)
        out = lax.dot_general(
            u, spread_matrix(), (((1,), (1,)), ((), ())), preferred_element_type=F32)
        sb[3, :, :, :, G:GE] = out.astype(BF16).reshape(4, 4, 16, 128)

    x0 = give(0)
    x1 = give(1)
    take(0, x0)
    x2 = give(2)
    take(1, x1)
    x3 = give(3)
    take(2, x2)
    take(3, x3)
    for k in range(2):
        rows = slice(k * TK, (k + 1) * TK)
        dl_v[rows] = jnp.transpose(dl_t[k].astype(F32)).astype(BF16)
        sc = scale_v[rows]
        coef_v[rows] = jnp.transpose(jnp.broadcast_to(inner[k], (128, TK))) * sc * sc
    q_end(0)
    hidden_block(0)
    hidden_block(1)
    q_end(1)
    hidden_block(2)
    p_end(0)
    hidden_block(3)
    q_end(2)
    p_end(1)
    z_begin(0)
    hidden_block(4)
    q_end(3)
    p_end(2)
    hidden_block(5)
    z_end(0)
    p_end(3)
    z_begin(1)
    hidden_block(6)
    hidden_block(7)
    z_end(1)

    for src in range(2):
        for ch in range(2):
            mine = (c == src) & (zl == c * 2 + ch)

            @pl.when(jnp.logical_not(mine))
            def _():
                pltpu.make_async_remote_copy(
                    src_ref=yv, dst_ref=fr.at[src, ch],
                    send_sem=fsend_sem.at[0], recv_sem=frecv_sem.at[src * 2 + ch],
                    device_id=sibling, device_id_type=MESH,
                ).wait_recv()
            for sub in range(2):
                start = src * HALF + ch * W + sub * G
                gw_ref[:, start:start + G] = fr[src, ch, sub * 4:sub * 4 + 4, 0:G]
    gains = fr[0, 1, :, G:GE] + fr[1, 1, :, G:GE]
    mine = jnp.zeros((2, 128), F32)
    for i in range(4):
        mine = jnp.where(w == i, gains[i * 2:i * 2 + 2], mine)
    gg_ref[...] = mine[:, 0:GN]

    for copy in started:
        copy.wait_send()

    @pl.when(edge)
    def _():
        for copy in z_gain + z_head[0] + z_head[1]:
            copy.wait_send()
    for j in range(2):
        for owner in range(4):
            target = (owner >> 1) * 4 + (owner & 1) * 2 + j

            @pl.when(target != z)
            def _():
                z_copy(j, owner).wait_send()

    for to in range(4):
        @pl.when(jnp.logical_not((zl == to) & (c == (zl >> 1))))
        def _():
            f_copy(to).wait_send()


def local(hidden, norm_gains, head_block, targets, rest_lse, cotangent):
    any_space = pl.BlockSpec(memory_space=pl.ANY)
    vmem = pl.BlockSpec(memory_space=pltpu.VMEM)
    scratch = [
        pltpu.VMEM((T, D), BF16),
        pltpu.VMEM((T, D), BF16),
        pltpu.VMEM((16, 16, D), BF16),
        pltpu.VMEM((4, 4, 2, 2, 16, G), BF16),
        pltpu.VMEM((4, 4, 2, 2, 16, G), BF16),
        pltpu.VMEM((2, 16, G), BF16),
        pltpu.VMEM((4, 8, 128), F32),
        pltpu.VMEM((4, 4, 8, 128), F32),
        pltpu.VMEM((2, 8, D), F32),
        pltpu.VMEM((T, 128), F32),
        pltpu.VMEM((2, V, TK), BF16),
        pltpu.VMEM((T, V), BF16),
        pltpu.VMEM((T, 128), F32),
        pltpu.VMEM((T, G), F32),
        pltpu.VMEM((16, 8, G), F32),
        pltpu.VMEM((2, 16, 16, G), F32),
        pltpu.VMEM((4, 16, 16, G), BF16),
        pltpu.VMEM((4, 16, 16, G), BF16),
        pltpu.VMEM((4, 4, 4, 16, GE), BF16),
        pltpu.VMEM((4, 3, 4, 16, GE), BF16),
        pltpu.VMEM((4, 4, 16, GE), BF16),
        pltpu.VMEM((4, 3, 16, GE), BF16),
        pltpu.VMEM((4, 16, GE), F32),
        pltpu.VMEM((2, 4, 8, GE), F32),
        pltpu.VMEM((8, 8, GE), F32),
        pltpu.VMEM((8, GE), F32),
        pltpu.VMEM((2, 2, 8, GE), F32),
        pltpu.SemaphoreType.DMA((4,)),
        pltpu.SemaphoreType.DMA((NSEM,)),
        pltpu.SemaphoreType.DMA((NSEM,)),
        pltpu.SemaphoreType.DMA((2, 4)),
        pltpu.SemaphoreType.DMA((8,)),
        pltpu.SemaphoreType.DMA((4,)),
        pltpu.SemaphoreType.DMA((4,)),
        pltpu.SemaphoreType.REGULAR((3,)),
    ]
    grad_hidden, grad_head, grad_gains = pl.pallas_call(
        kernel,
        out_shape=(pltpu.VMEM((T, D), BF16), pltpu.VMEM((4, D), F32), pltpu.VMEM((2, GN), F32)),
        in_specs=[any_space, vmem, vmem, vmem, vmem, vmem],
        out_specs=(vmem, vmem, vmem),
        scratch_shapes=scratch,
        compiler_params=pltpu.CompilerParams(
            collective_id=0, has_side_effects=True, vmem_limit_bytes=50 << 20),
        cost_estimate=pl.CostEstimate(
            flops=6 * T * D * V, bytes_accessed=4 * T * D, transcendentals=2 * T * V),
        name="head_backward",
    )(hidden.reshape(T, D), norm_gains, head_block, targets, rest_lse, cotangent)
    return grad_hidden.reshape(hidden.shape), grad_head, grad_gains


def solution(mesh):
    tokens = P(None, ("replica", "shard"))
    in_specs = (
        P(None, ("replica", "shard"), None),
        P(None, "shard"),
        P("shard", None),
        tokens,
        tokens,
        tokens,
    )
    out_specs = (P(None, ("replica", "shard"), None), P("shard", None), P(None, "shard"))
    return jax.shard_map(local, mesh=mesh, in_specs=in_specs, out_specs=out_specs, check_vma=False)
```

time: 86.4 us -> 73.7 us (0.85)
  Pallas kernels: 79 us -> 68.9 us
  local copies, waits for them, and re-layouts: 6.61 us -> 3.65 us
    pallas_call x1, Pallas kernels: 79 us -> 68.9 us  [local(): pl.pallas_call(kernel, out_shape=(pltpu.VMEM((T, D), BF16), pltpu.VMEM((4...]
    unnamed x7 -> x3, local copies, waits for them, and re-layouts: 6.61 us -> 3.65 us
where the time goes in v2:
time: 73.7 us; the launch traced here: 73.2 us
  Pallas kernels  68.9 us (93%)
  local copies, waits for them, and re-layouts  3.65 us (5%)
    pallas_call x1, Pallas kernels, local(): pl.pallas_call(kernel, out_shape=(pltpu.VMEM((T, D), BF16), pltpu.VMEM((4...  68.9 us
    unnamed x3, local copies, waits for them, and re-layouts  3.65 us

profile of v2, /device:TPU:1, one launch (start us, length us, event | category | flops | bytes accessed | tf_op | source)
XLA Modules:
  0.0 73.2 jit_solution(13952459823114221219)
XLA Ops:
  0.6 68.9 %head_backward.1 = (bf16[384,7168]{1,0:T(8,128)(2,1)S(1)}, f32[4,7168]{1,0:T(4,128)S(1)}, f32[2,112]{1,0:T(2,128)S(1)}) custom-call(bf16[384,7168]{1,0:T(8,128)(2,1)} %bitcast.3, bf16[2,112]{1,0:T(2,128)(2,1)} %gain_ref.1, bf16[4,7168]{1,0:T(4,128)(2,1)} %head_ref.1, s32[2,192]{1,0:T(2,128)} %tgt_ref.1, f32[2,192]{1,0:T(2,128)} %rest_ref.1, f32[2,192]{1,0:T(2,128)} %cot_ref.1), custom_call_target="tpu_custom_call" | custom-call | flops 4227858432 | bytes 11010048 | tf_op jit(solution)/shard_map/head_backward/pallas_call | solution.py:612
  69.6 2.4 %copy.12 = bf16[2,192,7168]{2,1,0:T(8,128)(2,1)} copy(bf16[2,192,7168]{2,1,0:T(8,128)(2,1)S(1)} %bitcast.2) | data formatting | bytes 11010048
  72.0 0.6 copy.14
  72.6 0.6 copy.13

commit v3 on v2

v3 whole, which is shorter than its diff:
```python
import jax
import jax.numpy as jnp
from jax import lax
from jax.experimental import pallas as pl
from jax.experimental.pallas import tpu as pltpu
from jax.sharding import PartitionSpec as P

eps = 1e-06
F32, BF16, I32 = jnp.float32, jnp.bfloat16, jnp.int32
MESH = pl.DeviceIdType.MESH

D = 7168
HALF = D // 2
G = 896
W = 2 * G
ZW = (G + 128) // 2
V = 256
TK = 192
T = 2 * TK
RT = 32
NRT = T // RT
GN = 112
NSEM = 112
SHARED = (0, 1, 2)


def iota(shape, dim):
    return lax.broadcasted_iota(I32, shape, dim)


def kernel(
    hid_ref, gain_ref, head_ref, tgt_ref, rest_ref, cot_ref,
    gx_ref, gw_ref, gg_ref,
    gain_v, head_v, tgt_v, rest_v, cot_v, xv, nv, hv, r_own, r_sib, raw, gcol, gblk, gfull, scale_v,
    dl_t, dl_v, coef_v, dn_v, gacc, gsb, gnq, gtb, gnp, gsum, xs, xr, sb, nq, zq, zf, nf, tb, npb,
    zsum, zp, zr, yv, fr,
    local_sem, send_sem, recv_sem, zsend_sem, zrecv_sem, fsend_sem, frecv_sem, near_sem,
):
    zl = lax.axis_index("replica")
    shard = lax.axis_index("shard")
    c = shard & 1
    zh = (shard >> 1) & 1
    x = (shard >> 2) & 3
    y = shard >> 4
    z = zh * 4 + zl
    pc = x + c * (y - x)
    qc = y + c * (x - y)

    def device(q, p, zz, cc):
        xx = p + c * (q - p)
        yy = q + c * (p - q)
        return (zz & 3, ((yy * 4 + xx) * 2 + (zz >> 2)) * 2 + cc)

    def at(dq=0, dp=0):
        return device((qc + dq) & 3, (pc + dp) & 3, z, c)

    def up(dz, cc=c):
        return device(qc, pc, (z + dz) & 7, cc)

    sibling = (zl, shard + 1 - 2 * c)

    count = [0]
    started = []

    def send(src, dst, target, start=True):
        i = count[0]
        count[0] += 1
        copy = pltpu.make_async_remote_copy(
            src_ref=src, dst_ref=dst, send_sem=send_sem.at[i], recv_sem=recv_sem.at[i],
            device_id=target, device_id_type=MESH,
        )
        if start:
            copy.start()
            started.append(copy)
        return copy

    barrier = pltpu.get_barrier_semaphore()
    first = [sibling, at(dp=1), at(dp=-1), at(dq=1), at(dq=-1)]
    for dz in (1, -1, 2, -2):
        first += [up(dz), up(dz, 1 - c)]
    for partner in first:
        pl.semaphore_signal(barrier, inc=1, device_id=partner, device_id_type=MESH)

    small_loads = []
    for i, (src, dst) in enumerate((
        (head_ref, head_v), (gain_ref, gain_v), (tgt_ref, tgt_v), (rest_ref, rest_v), (cot_ref, cot_v),
    )):
        copy = pltpu.make_async_copy(src, dst, local_sem.at[4 + i])
        copy.start()
        small_loads.append(copy)
    loads = []
    for i in range(4):
        rows = pl.ds(i * 96, 96)
        copy = pltpu.make_async_copy(hid_ref.at[rows], xv.at[rows], local_sem.at[i])
        copy.start()
        loads.append(copy)

    w = zh * 2 + c
    small_loads[0].wait()
    hb = head_v[...].astype(F32)
    for h in range(2):
        parts = [hb[:, (h * 4 + f) * G:(h * 4 + f + 1) * G] for f in range(4)]
        raw[h] = jnp.concatenate(parts, axis=0).astype(BF16)
    r_own[qc, pc, zh, c] = raw[c]
    small_loads[1].wait()
    gpad = jnp.concatenate([gain_v[...].astype(F32), jnp.zeros((2, 128 - GN), F32)], axis=1)
    gcol[w] = jnp.concatenate([gpad, jnp.zeros((6, 128), F32)], axis=0)

    pl.semaphore_wait(barrier, len(first))

    def relay(i, targets):
        for target in targets:
            pl.semaphore_signal(near_sem.at[i], inc=1, device_id=target, device_id_type=MESH)

    relay(0, [at(dp=1), at(dp=-1), at(dq=1), at(dq=-1), up(1), up(-1)])

    edge = (zl == 0) | (zl == 3)
    step = jnp.where(zl == 3, 1, -1)
    m_h = send(raw.at[1 - c], r_own.at[pc, qc, zh, c], sibling)
    m_g = send(gcol.at[w], gcol.at[w], sibling)
    z_head = []
    for d in (1, 2):
        z_head.append([
            send(raw.at[c], r_own.at[qc, pc, zh, c], up(d * step), start=False),
            send(raw.at[1 - c], r_own.at[pc, qc, zh, c], up(d * step, 1 - c), start=False),
        ])

    @pl.when(edge)
    def _():
        for copy in z_head[1] + z_head[0]:
            copy.start()

    def plane(d):
        return device(qc, pc, zh * 4 + ((zl + d) & 3), c)

    def far_begin():
        ref = r_own.at[qc, zl, zh]
        got["far"] = send(ref, ref, at(dq=2))

    def far_share():
        got["far"].wait_recv()
        ref = r_own.at[(qc - 2) & 3, zl, zh]
        for d in (1, 3, 2):
            got["share", d] = send(ref, ref, plane(d))

    def far_arrives():
        for d in (1, 3, 2):
            got["share", d].wait_recv()
        to_sibling(zh, 2)

    def z_arrives(near, far):
        @pl.when(edge)
        def _():
            for copy in near:
                copy.wait_recv()

        @pl.when(jnp.logical_not(edge))
        def _():
            for copy in far:
                copy.wait_recv()

    got = {}

    def along_q(k, dp):
        ref = r_own.at[qc, (pc + dp) & 3, k]
        for d in (1, 3) if k is zh else (1, 3, 2):
            got[k is zh, "q", dp, d] = send(ref, ref, at(dq=d))

    def begin(k):
        ref = r_own.at[qc, pc, k]
        for d in (1, 3, 2):
            got[k is zh, "p", d] = send(ref, ref, at(dp=d))

    def p_arrives(k, d):
        got[k is zh, "p", d].wait_recv()
        along_q(k, -d)

    def to_sibling(k, d):
        ref = r_own.at[(qc - d) & 3, :, k]
        got["sibling", d, k is zh] = send(ref, r_sib.at[(qc - d) & 3, :, k], sibling)

    def from_sibling(d):
        for key in list(got):
            if key[0] == "sibling" and key[1] == d:
                got[key].wait_recv()
        place(r_sib, 1 - c, 1 - c, pc - d)

    def q_arrives(k, d):
        for dp in (0, -1, -3, -2):
            got[k is zh, "q", dp, d].wait_recv()
            if d == 2:
                ref = r_own.at[(qc - d) & 3, (pc + dp) & 3, k]
                dst = r_sib.at[(qc - d) & 3, (pc + dp) & 3, k]
                got["sibling", d, k is zh, dp] = send(ref, dst, sibling)
        if d != 2:
            to_sibling(k, d)

    def scale_tiles(begin_tile, end_tile):
        def body(i, carry):
            rows = pl.ds(pl.multiple_of(i * RT, RT), RT)
            total = jnp.zeros((RT, 128), F32)
            for j in range(D // G):
                part = xv[rows, j * G:(j + 1) * G].astype(F32)
                part = part * part
                for l in range(G // 128):
                    total += part[:, l * 128:(l + 1) * 128]
            mean = jnp.sum(total, axis=1, keepdims=True) * (1.0 / D)
            scale_v[rows] = jnp.broadcast_to(lax.rsqrt(mean + eps), (RT, 128))
            return carry
        lax.fori_loop(begin_tile, end_tile, body, 0)

    def lanes(v):
        return jnp.concatenate([v] * (G // 128), axis=1)

    def normed_tiles(begin_tile, end_tile):
        def body(i, carry):
            rows = pl.ds(pl.multiple_of(i * RT, RT), RT)
            k = jnp.where(i >= NRT // 2, 1, 0)
            s = lanes(scale_v[rows])
            for j in range(D // G):
                cols = slice(j * G, (j + 1) * G)
                g = gfull[k, :, cols]
                g = jnp.concatenate([g] * (RT // 8), axis=0)
                nv[rows, cols] = (xv[rows, cols].astype(F32) * s * g).astype(BF16)
            return carry
        lax.fori_loop(begin_tile, end_tile, body, 0)

    def spread_matrix():
        j = iota((128, G), 0)
        col = iota((128, G), 1)
        hit = jnp.zeros((128, G), jnp.bool_)
        for m in range(8):
            hit = hit | (col == j + GN * m)
        return jnp.where(hit & (j < GN), 1.0, 0.0).astype(BF16)

    def inside(rows, shift):
        r = iota((rows, G), 0)
        p = (r >> shift) & 3
        q = r >> (shift + 2)
        xx = p + c * (q - p)
        m = (xx & 1) * 4 + ((r >> 1) & 3)
        col = iota((rows, G), 1)
        return (col >= m * GN) & (col < (m + 1) * GN)

    def make_gains():
        lhs = gblk[...].reshape(128, 128).astype(BF16)
        u = jnp.dot(lhs, spread_matrix(), preferred_element_type=F32)
        u = jnp.where(inside(128, 3), u, 0.0).astype(BF16)
        o = iota((16, 128), 0)
        i = iota((16, 128), 1)
        p = (i >> 3) & 3
        q = i >> 5
        xx = p + c * (q - p)
        yy = q + c * (p - q)
        sel = ((yy * 2 + (xx >> 1)) == (o >> 1)) & ((i & 1) == (o & 1))
        full = jnp.dot(jnp.where(sel, 1.0, 0.0).astype(BF16), u, preferred_element_type=F32)
        for j in range(8):
            for k in range(2):
                row = full[2 * j + k:2 * j + k + 1]
                gfull[k, :, j * G:(j + 1) * G] = jnp.broadcast_to(row, (8, G))

    def permutation():
        o = iota((V, V), 0)
        i = iota((V, V), 1)
        src = ((o >> 4) & 3) * 64 + ((o >> 2) & 3) * 16 + (o >> 6) * 4 + (o & 3)
        return jnp.where(i == src, 1.0, 0.0).astype(BF16)

    def place(buf, half, core, q):
        q = q & 3
        rows = jnp.dot(permutation(), buf[q].reshape(V, G), preferred_element_type=F32).astype(BF16)
        for f in range(4):
            cols = pl.ds(pl.multiple_of(half * HALF + f * G, 128), G)
            for p in range(4):
                yy = q + core * (p - q)
                xx = p + core * (q - p)
                hv[yy * 4 + xx, :, cols] = rows[f * 64 + p * 16:f * 64 + (p + 1) * 16]

    other = 1 - zh
    pl.semaphore_wait(near_sem.at[0], 6)
    relay(1, [up(1), up(-1)])
    m_h.wait_recv()
    begin(zh)
    along_q(zh, 0)
    m_g.wait_recv()
    pair = gcol.at[pl.ds(zh * 2, 2)]
    z_gain = [send(pair, pair, up(d * step), start=False) for d in (1, 2)]

    @pl.when(edge)
    def _():
        for copy in z_gain:
            copy.start()

    loads[0].wait()
    scale_tiles(0, 3)
    z_arrives(z_head[0], z_head[1])
    begin(other)
    for d in (1, 3, 2):
        p_arrives(zh, d)
    far_begin()
    along_q(other, 0)
    to_sibling(zh, 0)
    z_arrives(z_gain[:1], z_gain[1:])
    gblk[qc, pc] = jnp.concatenate([gcol[i][0:2] for i in range(4)], axis=0)
    g_p = [send(gblk.at[qc, pc], gblk.at[qc, pc], at(dp=d)) for d in (1, 3, 2)]
    loads[1].wait()
    scale_tiles(3, 6)
    for d in (1, 3, 2):
        p_arrives(other, d)
    to_sibling(other, 0)
    for copy in g_p:
        copy.wait_recv()
    g_q = [send(gblk.at[qc], gblk.at[qc], at(dq=d)) for d in (1, 3, 2)]
    pl.semaphore_wait(near_sem.at[1], 2)
    loads[2].wait()
    loads[3].wait()
    scale_tiles(6, 12)
    far_share()
    for d in (1, 3):
        q_arrives(zh, d)
    for copy in g_q:
        copy.wait_recv()
    make_gains()
    place(r_own, c, c, qc)
    from_sibling(0)
    normed_tiles(0, 4)
    far_arrives()
    normed_tiles(4, 8)
    q_arrives(other, 1)
    place(r_own, c, c, qc - 1)
    normed_tiles(8, 12)
    q_arrives(other, 3)
    place(r_own, c, c, qc - 3)
    from_sibling(1)
    q_arrives(other, 2)
    place(r_own, c, c, qc - 2)
    from_sibling(3)

    def logits_part(half, k):
        total = None
        for j in range(2):
            cols = pl.ds(pl.multiple_of(half * HALF + j * W, 128), W)
            part = lax.dot_general(
                hv[:, :, cols].reshape(V, W), nv[k * TK:(k + 1) * TK, cols],
                (((1,), (1,)), ((), ())), preferred_element_type=F32)
            total = part if total is None else total + part
        return total

    first_half = [logits_part(c, k) for k in range(2)]
    from_sibling(2)

    for copy in small_loads[2:]:
        copy.wait()
    inner = []
    for k in range(2):
        logits = first_half[k] + logits_part(1 - c, k)
        total = jnp.log(jnp.exp(rest_v[k:k + 1]) + jnp.sum(jnp.exp(logits), axis=0, keepdims=True))
        onehot = jnp.where(tgt_v[k:k + 1] == iota((V, TK), 0), 1.0, 0.0)
        grad = (cot_v[k:k + 1] * (jnp.exp(logits - total) - onehot)).astype(BF16)
        dl_t[k] = grad
        inner.append(jnp.sum(grad.astype(F32) * logits, axis=0, keepdims=True) * (1.0 / D))

    def partial(cols, k):
        return jnp.dot(dl_t[k], nv[k * TK:(k + 1) * TK, cols], preferred_element_type=F32)

    def block_cols(half, s):
        return pl.ds(pl.multiple_of(half * HALF + s * G, 128), G)

    def give(s):
        cols = block_cols(1 - c, s)
        xs[s] = (partial(cols, 0) + partial(cols, 1)).astype(BF16).reshape(16, 16, G)
        return send(xs.at[s], xr.at[s], sibling)

    def take(s, copy):
        cols = block_cols(c, s)
        own = partial(cols, 0) + partial(cols, 1)
        copy.wait_recv()
        for e in range(16):
            yy, xx = e >> 2, e & 3
            q, p = yy + c * (xx - yy), xx + c * (yy - xx)
            sb[s, q, p] = (own[e * 16:(e + 1) * 16] + xr[s, e].astype(F32)).astype(BF16)
        if s in SHARED:
            for d in (1, 3, 2):
                got["rz", s, d] = send(
                    sb.at[s, (qc + 2) & 3, (zl + d) & 3], zq.at[s, d - 1], plane(d))
        for d in (1, 3) if s in SHARED else (2, 1, 3):
            got["rq", s, d] = send(sb.at[s, (qc + d) & 3], nq.at[s, d - 1], at(dq=d))

    def far_sum(s):
        total = sb[s, (qc + 2) & 3, zl].astype(F32)
        for d in (1, 3, 2):
            got["rz", s, d].wait_recv()
            total = total + zq[s, d - 1].astype(F32)
        zf[s] = total.astype(BF16)
        got["rq", s, 2] = send(zf.at[s], nf.at[s], at(dq=2))

    def q_end(s):
        for d in (1, 3, 2):
            got["rq", s, d].wait_recv()
        for p in range(4):
            total = sb[s, qc, p].astype(F32)
            for d in (0, 2) if s in SHARED else range(3):
                total = total + nq[s, d, p].astype(F32)
            if s in SHARED:
                total = total + jnp.where(p == zl, nf[s].astype(F32), 0.0)
            tb[s, p] = total.astype(BF16)
        for d in (2, 1, 3):
            got["rp", s, d] = send(tb.at[s, (pc + d) & 3], npb.at[s, d - 1], at(dp=d))

    def p_end(s):
        for d in (1, 3, 2):
            got["rp", s, d].wait_recv()
        total = tb[s, pc].astype(F32)
        for d in range(3):
            total = total + npb[s, d].astype(F32)
        zsum[s] = total

    def gains_blocks():
        def body(j, carry):
            cols = pl.ds(pl.multiple_of(j * G, 128), G)
            hf = hv[:, :, cols].astype(F32).reshape(V // 8, 8, G)
            for k in range(2):
                part = partial(cols, k).reshape(V // 8, 8, G)
                gacc[j * 2 + k] = jnp.sum(hf * part, axis=0) / gfull[k, :, cols]
            return carry
        lax.fori_loop(0, 8, body, 0)

    def rider_begin():
        full = jnp.concatenate(
            [jnp.sum(gacc[i], axis=0, keepdims=True) for i in range(16)], axis=0).astype(BF16)
        o = iota((V, 16), 0)
        i = iota((V, 16), 1)
        p = (o >> 4) & 3
        q = o >> 6
        xx = p + c * (q - p)
        yy = q + c * (p - q)
        sel = ((yy * 2 + (xx >> 1)) == (i >> 1)) & ((o & 1) == (i & 1)) & ((o & 15) < 8)
        u = jnp.dot(jnp.where(sel, 1.0, 0.0).astype(BF16), full, preferred_element_type=F32)
        u = jnp.where(inside(V, 4), u, 0.0).astype(BF16)
        out = lax.dot_general(
            u, spread_matrix(), (((1,), (1,)), ((), ())), preferred_element_type=F32)
        gsb[...] = out.astype(BF16).reshape(4, 4, 16, 128)
        for d in (2, 1, 3):
            got["gq", d] = send(gsb.at[(qc + d) & 3], gnq.at[d - 1], at(dq=d))

    def rider_turn():
        for d in (1, 3, 2):
            got["gq", d].wait_recv()
        total = gsb[qc].astype(F32)
        for d in range(3):
            total = total + gnq[d].astype(F32)
        gtb[...] = total.astype(BF16)
        for d in (2, 1, 3):
            got["gp", d] = send(gtb.at[(pc + d) & 3], gnp.at[d - 1], at(dp=d))

    def rider_end():
        for d in (1, 3, 2):
            got["gp", d].wait_recv()
        total = gtb[pc].astype(F32)
        for d in range(3):
            total = total + gnp[d].astype(F32)
        gsum[...] = total

    def z_copy(j, owner):
        target = (owner >> 1) * 4 + (owner & 1) * 2 + j
        return pltpu.make_async_remote_copy(
            src_ref=zp.at[j, owner], dst_ref=zr.at[z],
            send_sem=zsend_sem.at[j, owner], recv_sem=zrecv_sem.at[z],
            device_id=device(qc, pc, target, c), device_id_type=MESH,
        )

    def z_begin(j):
        tail = gsum[0:8] if j == 1 else jnp.zeros((8, 128), F32)
        for owner in range(4):
            rows = slice(owner * 4, owner * 4 + 4)
            two = jnp.concatenate([zsum[2 * j, rows, 0:G], zsum[2 * j + 1, rows, 0:G]], axis=0)
            two = jnp.concatenate([two, tail], axis=1)
            zp[j, owner] = jnp.concatenate([two[:, 0:ZW], two[:, ZW:2 * ZW]], axis=0).astype(BF16)
        for owner in range(4):
            target = (owner >> 1) * 4 + (owner & 1) * 2 + j
            copy = z_copy(j, owner)

            @pl.when(target != z)
            def _():
                copy.start()

            @pl.when(target == z)
            def _():
                zr[z] = zp[j, owner]

    def f_copy(to):
        return pltpu.make_async_remote_copy(
            src_ref=yv, dst_ref=fr.at[c, zl & 1],
            send_sem=fsend_sem.at[to], recv_sem=frecv_sem.at[c * 2 + (zl & 1)],
            device_id=device(qc, pc, zh * 4 + to, zl >> 1), device_id_type=MESH,
        )

    def z_end(j):
        @pl.when((zl & 1) == j)
        def _():
            for src in range(8):
                @pl.when(src != z)
                def _():
                    pltpu.make_async_remote_copy(
                        src_ref=zp.at[j, 0], dst_ref=zr.at[src],
                        send_sem=zsend_sem.at[j, 0], recv_sem=zrecv_sem.at[src],
                        device_id=sibling, device_id_type=MESH,
                    ).wait_recv()
            total = zr[0].astype(F32)
            for src in range(1, 8):
                total = total + zr[src].astype(F32)
            yv[...] = total.astype(BF16)
            for to in (0, 3, 1, 2):
                mine = (zl == to) & (c == (zl >> 1))

                @pl.when(jnp.logical_not(mine))
                def _():
                    f_copy(to).start()

                @pl.when(mine)
                def _():
                    fr[c, zl & 1] = yv[...]

    def hidden_block(j):
        cols = slice(j * G, (j + 1) * G)
        dn_v[...] = jnp.dot(dl_v[...], hv[:, :, cols].reshape(V, G), preferred_element_type=F32)
        for k in range(2):
            g = jnp.concatenate([gfull[k, :, cols]] * (RT // 8), axis=0)

            def body(i, carry):
                rows = pl.ds(pl.multiple_of(i * RT, RT), RT)
                gx_ref[rows, cols] = (
                    lanes(scale_v[rows]) * g * dn_v[rows]
                    - xv[rows, cols].astype(F32) * lanes(coef_v[rows])
                ).astype(BF16)
                return carry
            lax.fori_loop(k * NRT // 2, (k + 1) * NRT // 2, body, 0)

    x0 = give(0)
    x1 = give(1)
    x2 = give(2)
    take(0, x0)
    x3 = give(3)
    take(1, x1)
    take(2, x2)
    take(3, x3)
    gains_blocks()
    rider_begin()
    for k in range(2):
        rows = slice(k * TK, (k + 1) * TK)
        dl_v[rows] = jnp.transpose(dl_t[k].astype(F32)).astype(BF16)
        sc = scale_v[rows]
        coef_v[rows] = jnp.transpose(jnp.broadcast_to(inner[k], (128, TK))) * sc * sc
    for i in SHARED:
        far_sum(i)
    hidden_block(0)
    hidden_block(1)
    q_end(0)
    rider_turn()
    hidden_block(2)
    q_end(1)
    hidden_block(3)
    q_end(2)
    p_end(0)
    q_end(3)
    p_end(1)
    z_begin(0)
    hidden_block(4)
    rider_end()
    p_end(2)
    hidden_block(5)
    p_end(3)
    z_begin(1)
    z_end(0)
    hidden_block(6)
    hidden_block(7)
    z_end(1)

    for src in range(2):
        for ch in range(2):
            mine = (c == src) & (zl == c * 2 + ch)

            @pl.when(jnp.logical_not(mine))
            def _():
                pltpu.make_async_remote_copy(
                    src_ref=yv, dst_ref=fr.at[src, ch],
                    send_sem=fsend_sem.at[0], recv_sem=frecv_sem.at[src * 2 + ch],
                    device_id=sibling, device_id_type=MESH,
                ).wait_recv()
            both = fr[src, ch].astype(F32)
            for sub in range(2):
                start = src * HALF + ch * W + sub * G
                gw_ref[:, start:start + ZW] = both[sub * 4:sub * 4 + 4]
                gw_ref[:, start + ZW:start + G] = both[8 + sub * 4:12 + sub * 4, 0:G - ZW]
    gains = fr[0, 1].astype(F32)[8:16, G - ZW:ZW] + fr[1, 1].astype(F32)[8:16, G - ZW:ZW]
    mine = jnp.zeros((2, 128), F32)
    for i in range(4):
        mine = jnp.where(w == i, gains[i * 2:i * 2 + 2], mine)
    gg_ref[...] = mine[:, 0:GN]

    for copy in started:
        copy.wait_send()

    @pl.when(edge)
    def _():
        for copy in z_gain + z_head[0] + z_head[1]:
            copy.wait_send()
    for j in range(2):
        for owner in range(4):
            target = (owner >> 1) * 4 + (owner & 1) * 2 + j

            @pl.when(target != z)
            def _():
                z_copy(j, owner).wait_send()

    for to in range(4):
        @pl.when(jnp.logical_not((zl == to) & (c == (zl >> 1))))
        def _():
            f_copy(to).wait_send()


def place_results(gx, gw, gg, gx_out, gw_out, gg_out, sem):
    copies = [
        pltpu.make_async_copy(gw, gw_out, sem.at[0]),
        pltpu.make_async_copy(gg, gg_out, sem.at[1]),
    ]
    for i in range(4):
        part = gx_out.at[i // 2, pl.ds(i % 2 * 96, 96)]
        copies.append(pltpu.make_async_copy(gx.at[i // 2, pl.ds(i % 2 * 96, 96)], part, sem.at[2 + i]))
    for copy in copies:
        copy.start()
    for copy in copies:
        copy.wait()


def local(hidden, norm_gains, head_block, targets, rest_lse, cotangent):
    any_space = pl.BlockSpec(memory_space=pl.ANY)
    vmem = pl.BlockSpec(memory_space=pltpu.VMEM)
    scratch = [
        pltpu.VMEM((2, GN), BF16),
        pltpu.VMEM((4, D), BF16),
        pltpu.VMEM((2, TK), I32),
        pltpu.VMEM((2, TK), F32),
        pltpu.VMEM((2, TK), F32),
        pltpu.VMEM((T, D), BF16),
        pltpu.VMEM((T, D), BF16),
        pltpu.VMEM((16, 16, D), BF16),
        pltpu.VMEM((4, 4, 2, 2, 16, G), BF16),
        pltpu.VMEM((4, 4, 2, 2, 16, G), BF16),
        pltpu.VMEM((2, 16, G), BF16),
        pltpu.VMEM((4, 8, 128), F32),
        pltpu.VMEM((4, 4, 8, 128), F32),
        pltpu.VMEM((2, 8, D), F32),
        pltpu.VMEM((T, 128), F32),
        pltpu.VMEM((2, V, TK), BF16),
        pltpu.VMEM((T, V), BF16),
        pltpu.VMEM((T, 128), F32),
        pltpu.VMEM((T, G), F32),
        pltpu.VMEM((16, 8, G), F32),
        pltpu.VMEM((4, 4, 16, 128), BF16),
        pltpu.VMEM((3, 4, 16, 128), BF16),
        pltpu.VMEM((4, 16, 128), BF16),
        pltpu.VMEM((3, 16, 128), BF16),
        pltpu.VMEM((16, 128), F32),
        pltpu.VMEM((4, 16, 16, G), BF16),
        pltpu.VMEM((4, 16, 16, G), BF16),
        pltpu.VMEM((4, 4, 4, 16, G), BF16),
        pltpu.VMEM((4, 3, 4, 16, G), BF16),
        pltpu.VMEM((3, 3, 16, G), BF16),
        pltpu.VMEM((3, 16, G), BF16),
        pltpu.VMEM((3, 16, G), BF16),
        pltpu.VMEM((4, 4, 16, G), BF16),
        pltpu.VMEM((4, 3, 16, G), BF16),
        pltpu.VMEM((4, 16, G), F32),
        pltpu.VMEM((2, 4, 16, ZW), BF16),
        pltpu.VMEM((8, 16, ZW), BF16),
        pltpu.VMEM((16, ZW), BF16),
        pltpu.VMEM((2, 2, 16, ZW), BF16),
        pltpu.SemaphoreType.DMA((9,)),
        pltpu.SemaphoreType.DMA((NSEM,)),
        pltpu.SemaphoreType.DMA((NSEM,)),
        pltpu.SemaphoreType.DMA((2, 4)),
        pltpu.SemaphoreType.DMA((8,)),
        pltpu.SemaphoreType.DMA((4,)),
        pltpu.SemaphoreType.DMA((4,)),
        pltpu.SemaphoreType.REGULAR((2,)),
    ]
    grad_hidden, grad_head, grad_gains = pl.pallas_call(
        kernel,
        out_shape=(pltpu.VMEM((T, D), BF16), pltpu.VMEM((4, D), F32), pltpu.VMEM((2, GN), F32)),
        in_specs=[any_space] * 6,
        out_specs=(vmem, vmem, vmem),
        scratch_shapes=scratch,
        compiler_params=pltpu.CompilerParams(
            collective_id=0, has_side_effects=True, vmem_limit_bytes=50 << 20),
        cost_estimate=pl.CostEstimate(
            flops=6 * T * D * V, bytes_accessed=4 * T * D, transcendentals=2 * T * V),
        name="head_backward",
    )(hidden.reshape(T, D), norm_gains, head_block, targets, rest_lse, cotangent)
    return pl.pallas_call(
        place_results,
        out_shape=(
            jax.ShapeDtypeStruct(hidden.shape, BF16),
            jax.ShapeDtypeStruct((4, D), F32),
            jax.ShapeDtypeStruct((2, GN), F32),
        ),
        in_specs=[vmem] * 3,
        out_specs=(any_space,) * 3,
        scratch_shapes=[pltpu.SemaphoreType.DMA((6,))],
        compiler_params=pltpu.CompilerParams(vmem_limit_bytes=16 << 20),
        name="place_results",
    )(*[pltpu.with_memory_space_constraint(v, pltpu.VMEM)
        for v in (grad_hidden.reshape(hidden.shape), grad_head, grad_gains)])


def solution(mesh):
    tokens = P(None, ("replica", "shard"))
    in_specs = (
        P(None, ("replica", "shard"), None),
        P(None, "shard"),
        P("shard", None),
        tokens,
        tokens,
        tokens,
    )
    out_specs = (P(None, ("replica", "shard"), None), P("shard", None), P(None, "shard"))
    return jax.shard_map(local, mesh=mesh, in_specs=in_specs, out_specs=out_specs, check_vma=False)
```

time: 73.7 us -> 68.3 us (0.927)
  local copies, waits for them, and re-layouts: 3.65 us -> 0 us
  Pallas kernels: 68.9 us -> 67.5 us
    pallas_call x1, Pallas kernels: 68.9 us -> 65 us  [local(): pl.pallas_call(kernel, out_shape=(pltpu.VMEM((T, D), BF16), pltpu.VMEM((4...]
    unnamed x3 -> x0, local copies, waits for them, and re-layouts: 3.65 us -> none
    pallas_call x0 -> x1, Pallas kernels: none -> 2.53 us  [local(): pl.pallas_call(place_results, out_shape=(jax.ShapeDtypeStruct(hidden.shap...]
where the time goes in v3:
time: 68.3 us; the launch traced here: 68.2 us
  Pallas kernels  67.5 us (99%)
    pallas_call x1, Pallas kernels, local(): pl.pallas_call(kernel, out_shape=(pltpu.VMEM((T, D), BF16), pltpu.VMEM((4...  65 us
    pallas_call x1, Pallas kernels, local(): pl.pallas_call(place_results, out_shape=(jax.ShapeDtypeStruct(hidden.shap...  2.53 us

profile of v3, /device:TPU:1, one launch (start us, length us, event | category | flops | bytes accessed | tf_op | source)
XLA Modules:
  0.0 68.2 jit_solution(15864694195739762944)
XLA Ops:
  0.6 65.0 %head_backward.1 = (bf16[384,7168]{1,0:T(8,128)(2,1)S(1)}, f32[4,7168]{1,0:T(4,128)S(1)}, f32[2,112]{1,0:T(2,128)S(1)}) custom-call(bf16[384,7168]{1,0:T(8,128)(2,1)} %bitcast.3, bf16[2,112]{1,0:T(2,128)(2,1)} %gain_ref.1, bf16[4,7168]{1,0:T(4,128)(2,1)} %head_ref.1, s32[2,192]{1,0:T(2,128)} %tgt_ref.1, f32[2,192]{1,0:T(2,128)} %rest_ref.1, f32[2,192]{1,0:T(2,128)} %cot_ref.1), custom_call_target="tpu_custom_call" | custom-call | flops 4227858432 | bytes 11010048 | tf_op jit(solution)/shard_map/head_backward/pallas_call | solution.py:687
  65.6 2.5 %place_results.1 = (bf16[2,192,7168]{2,1,0:T(8,128)(2,1)}, f32[4,7168]{1,0:T(4,128)}, f32[2,112]{1,0:T(2,128)}) custom-call(bf16[2,192,7168]{2,1,0:T(8,128)(2,1)S(1)} %bitcast.2, f32[4,7168]{1,0:T(4,128)S(1)} %get-tuple-element.7.gw, f32[2,112]{1,0:T(2,128)S(1)} %get-tuple-element.8.gg), custom_call_target="tpu_custom_call" | custom-call | tf_op jit(solution)/shard_map/place_results/pallas_call | solution.py:699

commit v4 on v3

--- a/solution.py
+++ b/solution.py
@@ -173,6 +173,8 @@
 
     def p_arrives(k, d):
         got[k is zh, "p", d].wait_recv()
+        if k is zh and d == 2:
+            far_begin()
         along_q(k, -d)
 
     def to_sibling(k, d):
@@ -296,7 +298,6 @@
     begin(other)
     for d in (1, 3, 2):
         p_arrives(zh, d)
-    far_begin()
     along_q(other, 0)
     to_sibling(zh, 0)
     z_arrives(z_gain[:1], z_gain[1:])
@@ -460,8 +461,14 @@
             total = total + gnp[d].astype(F32)
         gsum[...] = total
 
+    def z_owner(j, owner):
+        core = owner & 1
+        return (owner >> 1) * 4 + (1 + core if j else 3 * core)
+
+    mine_j = ((zl + 1) >> 1) & 1
+
     def z_copy(j, owner):
-        target = (owner >> 1) * 4 + (owner & 1) * 2 + j
+        target = z_owner(j, owner)
         return pltpu.make_async_remote_copy(
             src_ref=zp.at[j, owner], dst_ref=zr.at[z],
             send_sem=zsend_sem.at[j, owner], recv_sem=zrecv_sem.at[z],
@@ -476,7 +483,7 @@
             two = jnp.concatenate([two, tail], axis=1)
             zp[j, owner] = jnp.concatenate([two[:, 0:ZW], two[:, ZW:2 * ZW]], axis=0).astype(BF16)
         for owner in range(4):
-            target = (owner >> 1) * 4 + (owner & 1) * 2 + j
+            target = z_owner(j, owner)
             copy = z_copy(j, owner)
 
             @pl.when(target != z)
@@ -487,15 +494,21 @@
             def _():
                 zr[z] = zp[j, owner]
 
+    def z_sent(j):
+        for owner in range(4):
+            @pl.when(z_owner(j, owner) != z)
+            def _():
+                z_copy(j, owner).wait_send()
+
     def f_copy(to):
         return pltpu.make_async_remote_copy(
-            src_ref=yv, dst_ref=fr.at[c, zl & 1],
-            send_sem=fsend_sem.at[to], recv_sem=frecv_sem.at[c * 2 + (zl & 1)],
+            src_ref=yv, dst_ref=fr.at[c, mine_j],
+            send_sem=fsend_sem.at[to], recv_sem=frecv_sem.at[c * 2 + mine_j],
             device_id=device(qc, pc, zh * 4 + to, zl >> 1), device_id_type=MESH,
         )
 
     def z_end(j):
-        @pl.when((zl & 1) == j)
+        @pl.when(mine_j == j)
         def _():
             for src in range(8):
                 @pl.when(src != z)
@@ -518,7 +531,7 @@
 
                 @pl.when(mine)
                 def _():
-                    fr[c, zl & 1] = yv[...]
+                    fr[c, mine_j] = yv[...]
 
     def hidden_block(j):
         cols = slice(j * G, (j + 1) * G)
@@ -573,11 +586,20 @@
     z_end(0)
     hidden_block(6)
     hidden_block(7)
+    for copy in started:
+        copy.wait_send()
+    started.clear()
+
+    @pl.when(edge)
+    def _():
+        for copy in z_gain + z_head[0] + z_head[1]:
+            copy.wait_send()
+    z_sent(0)
     z_end(1)
 
     for src in range(2):
         for ch in range(2):
-            mine = (c == src) & (zl == c * 2 + ch)
+            mine = (c == src) & ((zl >> 1) == c) & (mine_j == ch)
 
             @pl.when(jnp.logical_not(mine))
             def _():
@@ -597,21 +619,7 @@
         mine = jnp.where(w == i, gains[i * 2:i * 2 + 2], mine)
     gg_ref[...] = mine[:, 0:GN]
 
-    for copy in started:
-        copy.wait_send()
-
-    @pl.when(edge)
-    def _():
-        for copy in z_gain + z_head[0] + z_head[1]:
-            copy.wait_send()
-    for j in range(2):
-        for owner in range(4):
-            target = (owner >> 1) * 4 + (owner & 1) * 2 + j
-
-            @pl.when(target != z)
-            def _():
-                z_copy(j, owner).wait_send()
-
+    z_sent(1)
     for to in range(4):
         @pl.when(jnp.logical_not((zl == to) & (c == (zl >> 1))))
         def _():

time: 68.3 us -> 67.4 us (0.987)
  Pallas kernels: 67.5 us -> 66.7 us
    pallas_call x1, Pallas kernels: 65 us -> 64.2 us  [local(): pl.pallas_call(kernel, out_shape=(pltpu.VMEM((T, D), BF16), pltpu.VMEM((4...]
where the time goes in v4:
time: 67.4 us
  Pallas kernels  66.7 us (99%)
    pallas_call x1, Pallas kernels, local(): pl.pallas_call(kernel, out_shape=(pltpu.VMEM((T, D), BF16), pltpu.VMEM((4...  64.2 us
    pallas_call x1, Pallas kernels, local(): pl.pallas_call(place_results, out_shape=(jax.ShapeDtypeStruct(hidden.shap...  2.53 us

profile of v4, /device:TPU:1, one launch (start us, length us, event | category | flops | bytes accessed | tf_op | source)
XLA Modules:
  0.0 67.4 jit_solution(13301525066701660653)
XLA Ops:
  0.6 64.2 %head_backward.1 = (bf16[384,7168]{1,0:T(8,128)(2,1)S(1)}, f32[4,7168]{1,0:T(4,128)S(1)}, f32[2,112]{1,0:T(2,128)S(1)}) custom-call(bf16[384,7168]{1,0:T(8,128)(2,1)} %bitcast.3, bf16[2,112]{1,0:T(2,128)(2,1)} %gain_ref.1, bf16[4,7168]{1,0:T(4,128)(2,1)} %head_ref.1, s32[2,192]{1,0:T(2,128)} %tgt_ref.1, f32[2,192]{1,0:T(2,128)} %rest_ref.1, f32[2,192]{1,0:T(2,128)} %cot_ref.1), custom_call_target="tpu_custom_call" | custom-call | flops 4227858432 | bytes 11010048 | tf_op jit(solution)/shard_map/head_backward/pallas_call | solution.py:695
  64.8 2.5 %place_results.1 = (bf16[2,192,7168]{2,1,0:T(8,128)(2,1)}, f32[4,7168]{1,0:T(4,128)}, f32[2,112]{1,0:T(2,128)}) custom-call(bf16[2,192,7168]{2,1,0:T(8,128)(2,1)S(1)} %bitcast.2, f32[4,7168]{1,0:T(4,128)S(1)} %get-tuple-element.7.gw, f32[2,112]{1,0:T(2,128)S(1)} %get-tuple-element.8.gg), custom_call_target="tpu_custom_call" | custom-call | tf_op jit(solution)/shard_map/place_results/pallas_call | solution.py:707

commit v5 on v4

--- a/solution.py
+++ b/solution.py
@@ -31,7 +31,7 @@
 def kernel(
     hid_ref, gain_ref, head_ref, tgt_ref, rest_ref, cot_ref,
     gx_ref, gw_ref, gg_ref,
-    gain_v, head_v, tgt_v, rest_v, cot_v, xv, nv, hv, r_own, r_sib, raw, gcol, gblk, gfull, scale_v,
+    gain_v, head_v, tgt_v, rest_v, cot_v, perm, xv, nv, hv, r_own, r_sib, raw, gcol, gblk, gfull, scale_v,
     dl_t, dl_v, coef_v, dn_v, gacc, gsb, gnq, gtb, gnp, gsum, xs, xr, sb, nq, zq, zf, nf, tb, npb,
     zsum, zp, zr, yv, fr,
     local_sem, send_sem, recv_sem, zsend_sem, zrecv_sem, fsend_sem, frecv_sem, near_sem,
@@ -269,7 +269,7 @@
 
     def place(buf, half, core, q):
         q = q & 3
-        rows = jnp.dot(permutation(), buf[q].reshape(V, G), preferred_element_type=F32).astype(BF16)
+        rows = jnp.dot(perm[...], buf[q].reshape(V, G), preferred_element_type=F32).astype(BF16)
         for f in range(4):
             cols = pl.ds(pl.multiple_of(half * HALF + f * G, 128), G)
             for p in range(4):
@@ -292,6 +292,7 @@
         for copy in z_gain:
             copy.start()
 
+    perm[...] = permutation()
     loads[0].wait()
     scale_tiles(0, 3)
     z_arrives(z_head[0], z_head[1])
@@ -323,17 +324,15 @@
     make_gains()
     place(r_own, c, c, qc)
     from_sibling(0)
-    normed_tiles(0, 4)
+    normed_tiles(0, 12)
+    q_arrives(other, 1)
+    q_arrives(other, 3)
+    q_arrives(other, 2)
     far_arrives()
-    normed_tiles(4, 8)
-    q_arrives(other, 1)
     place(r_own, c, c, qc - 1)
-    normed_tiles(8, 12)
-    q_arrives(other, 3)
     place(r_own, c, c, qc - 3)
+    place(r_own, c, c, qc - 2)
     from_sibling(1)
-    q_arrives(other, 2)
-    place(r_own, c, c, qc - 2)
     from_sibling(3)
 
     def logits_part(half, k):
@@ -649,6 +648,7 @@
         pltpu.VMEM((2, TK), I32),
         pltpu.VMEM((2, TK), F32),
         pltpu.VMEM((2, TK), F32),
+        pltpu.VMEM((V, V), BF16),
         pltpu.VMEM((T, D), BF16),
         pltpu.VMEM((T, D), BF16),
         pltpu.VMEM((16, 16, D), BF16),

time: 67.4 us -> 67.3 us (level)
  no operation moved by 1% of the time
where the time goes in v5:
time: 67.3 us; the launch traced here: 67.2 us
  Pallas kernels  66.6 us (99%)
    pallas_call x1, Pallas kernels, local(): pl.pallas_call(kernel, out_shape=(pltpu.VMEM((T, D), BF16), pltpu.VMEM((4...  64 us
    pallas_call x1, Pallas kernels, local(): pl.pallas_call(place_results, out_shape=(jax.ShapeDtypeStruct(hidden.shap...  2.53 us

profile of v5, /device:TPU:1, one launch (start us, length us, event | category | flops | bytes accessed | tf_op | source)
XLA Modules:
  0.0 67.2 jit_solution(18084005194897083833)
XLA Ops:
  0.6 64.0 %head_backward.1 = (bf16[384,7168]{1,0:T(8,128)(2,1)S(1)}, f32[4,7168]{1,0:T(4,128)S(1)}, f32[2,112]{1,0:T(2,128)S(1)}) custom-call(bf16[384,7168]{1,0:T(8,128)(2,1)} %bitcast.3, bf16[2,112]{1,0:T(2,128)(2,1)} %gain_ref.1, bf16[4,7168]{1,0:T(4,128)(2,1)} %head_ref.1, s32[2,192]{1,0:T(2,128)} %tgt_ref.1, f32[2,192]{1,0:T(2,128)} %rest_ref.1, f32[2,192]{1,0:T(2,128)} %cot_ref.1), custom_call_target="tpu_custom_call" | custom-call | flops 4227858432 | bytes 11010048 | tf_op jit(solution)/shard_map/head_backward/pallas_call | solution.py:695
  64.7 2.5 %place_results.1 = (bf16[2,192,7168]{2,1,0:T(8,128)(2,1)}, f32[4,7168]{1,0:T(4,128)}, f32[2,112]{1,0:T(2,128)}) custom-call(bf16[2,192,7168]{2,1,0:T(8,128)(2,1)S(1)} %bitcast.2, f32[4,7168]{1,0:T(4,128)S(1)} %get-tuple-element.7.gw, f32[2,112]{1,0:T(2,128)S(1)} %get-tuple-element.8.gg), custom_call_target="tpu_custom_call" | custom-call | tf_op jit(solution)/shard_map/place_results/pallas_call | solution.py:707
